TPU v7x, 512 devices: a whole 4x4x16 slice. The times are simulated.
512 devices in a mesh: ctx: 16 (over x, z_hi, core), head: 32 (over y, z_lo).
Axes of the slice: x: 4, y: 4, z: 16 (z_hi: 2, z_lo: 8; z = z_hi * 8 + z_lo), core: 2. Of those that a mesh axis runs over, the one named last changes fastest.
Arguments:
- hidden: bfloat16 [2048, 7168], P('ctx', 'head'), may hold values from -6 to 6
- query_down: bfloat16 [7168, 1536], P('head'), may hold values from -0.0625 to 0.0625
- latent_down: bfloat16 [7168, 576], P('head'), may hold values from -0.0625 to 0.0625
- query_gain: float32 [1536], replicated, may hold values from 0.5 to 24, as said below
- latent_gain: float32 [512], replicated, may hold values from 0.25 to 1.75
- query_up: bfloat16 [1536, 24576], P(None, 'head'), may hold values from -0.15625 to 0.15625
- key_absorb: bfloat16 [512, 16384], P(None, 'head'), may hold values from -0.5 to 0.5
- value_absorb: bfloat16 [512, 16384], P(None, 'head'), may hold values from -1 to 1
- out_proj: bfloat16 [16384, 7168], P('head', 'ctx'), may hold values from -0.09375 to 0.09375
- doc_start: int32 [2048], P('ctx'), may hold values from 0 to 2047, as said below
- positions: int32 [2048], P('ctx'), may hold values from 0 to 2047, as said below
Outputs:
- attended: bfloat16 [2048, 7168], P('head', 'ctx')
Inputs may be any that keep to these rules, and one draw needn't show every extreme that they name: doc_start never falls along the window, doc_start[i] <= i, doc_start[0] = 0, doc_start[i] = i at the first token of every document, the first document covers at least the first 1152 tokens, and the last token of the window begins a document of its own. positions[i] = i - doc_start[i] in every document but the first; the first document began before the window, and its positions run on from an offset such that its last token has position 2047. `query_gain`: a positive gain for each channel.
All inputs are finite; a program needn't handle non-finite values.
Results may differ from a plain program's by a relative error of at most 0.027.
Values may be sent and summed in bfloat16 or wider, within the bound.
A program may use at most 64 MiB of HBM per device.

v0:
```python
import jax
import jax.numpy as jnp
from jax import lax
from jax.sharding import PartitionSpec as P

LATENT = 512
ROPE = 64
NOPE = 128
VDIM = 128


def rms_norm(values, gain):
    scale = lax.rsqrt(jnp.mean(values * values, axis=-1, keepdims=True) + 1e-06)
    return values * scale * gain


def rotate(values, angles_pos):
    half = values.shape[-1] // 2
    freqs = 10000.0 ** (-2.0 * jnp.arange(half, dtype=jnp.float32) / values.shape[-1])
    angles = angles_pos.astype(jnp.float32)[:, None] * freqs[None, :]
    if values.ndim == 3:
        angles = angles[:, None, :]
    first_half = values[..., :half]
    second_half = values[..., half:]
    cosine = jnp.cos(angles)
    sine = jnp.sin(angles)
    return jnp.concatenate(
        [first_half * cosine - second_half * sine, second_half * cosine + first_half * sine],
        axis=-1,
    )


def body(
    hidden,
    query_down,
    latent_down,
    query_gain,
    latent_gain,
    query_up,
    key_absorb,
    value_absorb,
    out_proj,
    doc_start,
    positions,
):
    tok_rows = hidden.shape[0]
    heads_here = query_up.shape[1] // (NOPE + ROPE)
    query_part = jnp.dot(hidden, query_down, preferred_element_type=jnp.float32)
    latent_part = jnp.dot(hidden, latent_down, preferred_element_type=jnp.float32)
    query_low, latent_raw = lax.psum((query_part, latent_part), "head")
    query_normed = rms_norm(query_low, query_gain).astype(jnp.bfloat16)
    latent = rms_norm(latent_raw[:, :LATENT], latent_gain).astype(jnp.bfloat16)
    key_rot = rotate(latent_raw[:, LATENT:], positions).astype(jnp.bfloat16)
    keys = jnp.concatenate([latent, key_rot], axis=1)
    query_full = jnp.dot(query_normed, query_up, preferred_element_type=jnp.float32).reshape(
        tok_rows, heads_here, NOPE + ROPE
    )
    query_nope = query_full[:, :, :NOPE].astype(jnp.bfloat16)
    query_rot = rotate(query_full[:, :, NOPE:], positions).astype(jnp.bfloat16)
    query_lat = jnp.einsum(
        "thn,lhn->thl",
        query_nope,
        key_absorb.reshape(LATENT, heads_here, NOPE),
        preferred_element_type=jnp.float32,
    ).astype(jnp.bfloat16)
    queries = jnp.concatenate([query_lat, query_rot], axis=2).reshape(
        tok_rows * heads_here, LATENT + ROPE
    )
    first_row = lax.axis_index("ctx") * tok_rows
    query_index = jnp.repeat(first_row + jnp.arange(tok_rows, dtype=jnp.int32), heads_here)
    query_doc = jnp.repeat(doc_start, heads_here)
    scale = (NOPE + ROPE) ** (-0.5)
    all_rows = tok_rows * heads_here
    piece = lax.all_gather(keys, "ctx", axis=0, tiled=True)
    running_max = jnp.full((all_rows,), -1e30, jnp.float32)
    key_index = jnp.arange(piece.shape[0], dtype=jnp.int32)
    scores = (
        lax.dot_general(
            queries, piece, (((1,), (1,)), ((), ())), preferred_element_type=jnp.float32
        )
        * scale
    )
    visible = (key_index[None, :] <= query_index[:, None]) & (
        key_index[None, :] >= query_doc[:, None]
    )
    scores = jnp.where(visible, scores, -1e30)
    new_max = jnp.maximum(running_max, jnp.max(scores, axis=1))
    expo = jnp.where(visible, jnp.exp(scores - new_max[:, None]), 0.0)
    total = jnp.sum(expo, axis=1)
    weighted = jnp.dot(
        expo.astype(jnp.bfloat16), piece[:, :LATENT], preferred_element_type=jnp.float32
    )
    running_max, total, weighted = (new_max, total, weighted)
    mixed = (weighted / total[:, None]).astype(jnp.bfloat16).reshape(tok_rows, heads_here, LATENT)
    head_out = jnp.einsum(
        "thl,lhv->thv",
        mixed,
        value_absorb.reshape(LATENT, heads_here, VDIM),
        preferred_element_type=jnp.float32,
    ).astype(jnp.bfloat16)
    head_out = head_out.reshape(tok_rows, heads_here * VDIM)
    partial_out = jnp.dot(
        lax.all_gather(head_out, "ctx", axis=0, tiled=True),
        out_proj,
        preferred_element_type=jnp.float32,
    )
    return lax.psum_scatter(partial_out, "head", scatter_dimension=0, tiled=True).astype(
        jnp.bfloat16
    )


def solution(mesh):
    in_specs = (
        P("ctx", "head"),
        P("head", None),
        P("head", None),
        P(),
        P(),
        P(None, "head"),
        P(None, "head"),
        P(None, "head"),
        P("head", "ctx"),
        P("ctx"),
        P("ctx"),
    )
    out_specs = P("head", "ctx")
    return jax.shard_map(body, mesh=mesh, in_specs=in_specs, out_specs=out_specs, check_vma=False)
```

profile of v0, /device:TPU:2, one launch (start us, length us, event | category | flops | bytes accessed | tf_op | source)
XLA Modules:
  0.0 914.1 jit_solution(12757778229068693633)
XLA Ops:
  6.6 2.5 fusion.27
  9.0 2.0 fusion.28
  11.1 0.7 convert_element_type.37
  11.8 452.7 %all-reduce.3.cloned.1.call-done = (f32[128,576]{0,1:T(8,128)}, f32[128,1536]{1,0:T(8,128)}) async-done(((f32[128,576]{0,1:T(8,128)}, f32[128,1536]{1,0:T(8,128)}), (f32[128,576]{0,1:T(8,128)}, f32[128,1536]{1,0:T(8,128)})) %all-reduce.3.cloned.1.call-update) | async-done | bytes 1081360 | tf_op jit(solution)/shard_map/psum | solution.py:50
  464.5 1.0 multiply_reduce_fusion.1
  465.5 0.9 multiply_cosine_fusion
  466.4 1.1 multiply_convert_fusion.2
  467.5 0.7 pad_maximum_fusion.1
  468.3 0.1 le.18
  468.5 0.1 ge.6
  468.7 1.0 copy.42
  469.7 1.3 multiply_reduce_fusion
  471.0 2.2 fusion.20
  473.2 0.1 copy.43
  473.3 0.1 copy.44
  473.5 0.1 copy.34
  473.6 0.1 copy.36
  473.7 0.1 subtract_convert_fusion
  473.7 1.4 fusion.12
  475.1 0.1 pad_maximum_fusion
  475.3 0.5 copy.37
  475.8 1.2 reshape.96
  477.0 84.5 %all-gather.3.cloned.1.call-done = bf16[2048,576]{0,1:T(8,128)(2,1)} async-done(((bf16[128,576]{0,1:T(8,128)(2,1)}), bf16[2048,576]{0,1:T(8,128)(2,1)}) %all-gather.3.cloned.1.call-update) | async-done | bytes 2359312 | tf_op jit(solution)/shard_map/all_gather | solution.py:74
  561.5 4.3 fusion.1
  565.8 2.1 fusion.2
  567.9 2.5 divide_convert_fusion
  570.5 0.9 reshape.97
  571.4 2.0 convolution_convert_fusion.1
  573.5 81.0 %all-gather.5.cloned.1.call-done = bf16[2048,512]{0,1:T(8,128)(2,1)} async-done(((bf16[128,512]{0,1:T(8,128)(2,1)}), bf16[2048,512]{0,1:T(8,128)(2,1)}) %all-gather.5.cloned.1.call-update) | async-done | bytes 2097168 | tf_op jit(solution)/shard_map/all_gather | solution.py:103
  654.5 4.9 fusion.29
  659.4 246.6 %reduce-scatter.2.cloned.1.call-done = f32[64,448]{1,0:T(8,128)} async-done(((f32[2048,448]{1,0:T(8,128)}), f32[64,448]{1,0:T(8,128)}) %reduce-scatter.2.cloned.1.call-update) | async-done | bytes 114704 | tf_op jit(solution)/shard_map/reduce_scatter | solution.py:107
  906.1 1.5 convert_element_type.43
  (28 shorter events, 0.4 us)
Async XLA Ops:
  6.5 464.4 %copy-start = (bf16[1536,768]{1,0:T(8,128)(2,1)S(1)}, bf16[1536,768]{1,0:T(8,128)(2,1)}, u32[]{:S(2)}) copy-start(bf16[1536,768]{1,0:T(8,128)(2,1)} %param.16) | copy-start | bytes 7077892
  6.5 461.9 %copy-start.4 = (s32[128]{0:T(128)S(1)}, s32[128]{0:T(128)}, u32[]{:S(2)}) copy-start(s32[128]{0:T(128)} %param.20) | copy-start | bytes 1540
  6.5 462.1 %copy-start.1 = (bf16[512,512]{1,0:T(8,128)(2,1)S(1)}, bf16[512,512]{1,0:T(8,128)(2,1)}, u32[]{:S(2)}) copy-start(bf16[512,512]{1,0:T(8,128)(2,1)} %param.18) | copy-start | bytes 1572868
  6.5 464.4 %copy-start.3 = (f32[1536]{0:T(1024)S(1)}, f32[1536]{0:T(1024)}, u32[]{:S(2)}) copy-start(f32[1536]{0:T(1024)} %param.14) | copy-start | bytes 18436
  6.5 457.9 %all-reduce.3.cloned.1.call-start = ((), (), s32[]{:S(2)}) async-start(), calls=%async_computation.4 | async-start | bytes 2162688 | tf_op jit(solution)/shard_map/psum | solution.py:50
  11.1 550.4 %all-gather.3.cloned.1.call-start = ((), (), s32[]{:S(2)}) async-start(), calls=%async_computation.1 | async-start | bytes 2506752 | tf_op jit(solution)/shard_map/all_gather | solution.py:74
  468.2 186.3 %all-gather.5.cloned.1.call-start = ((), (), s32[]{:S(2)}) async-start(), calls=%async_computation.2 | async-start | bytes 2228224 | tf_op jit(solution)/shard_map/all_gather | solution.py:103
  565.8 2.1 copy-start.5
  567.9 3.5 copy-start.2
  573.4 332.6 %reduce-scatter.2.cloned.1.call-start = ((), (), s32[]{:S(2)}) async-start(), calls=%async_computation.3 | async-start | bytes 4325376 | tf_op jit(solution)/shard_map/reduce_scatter | solution.py:107
Sparse Core Ops, SparseCore 0:
  11.2 453.2 all-reduce.2
  468.3 93.1 all-gather.2
  573.6 80.8 all-gather.4
  659.5 246.4 reduce-scatter.1
where the time goes:
time: 915 us; the launch traced here: 914 us
  waiting for transfers between devices  865 us (95%)
  matrix products  21.8 us (2%)
  between operations  13.3 us (1%)
  other arithmetic  9.49 us (1%)
    psum x1, waiting for transfers between devices, body(): query_low, latent_raw = lax.psum((query_part, latent_part), 'head')  453 us
    reduce_scatter x1, waiting for transfers between devices, body(): lax.psum_scatter(partial_out, 'head', scatter_dimension=0, tiled=True)  247 us
    all_gather x1, waiting for transfers between devices, body(): piece = lax.all_gather(keys, 'ctx', axis=0, tiled=True)  84.5 us
    all_gather x1, waiting for transfers between devices, body(): lax.all_gather(head_out, 'ctx', axis=0, tiled=True)  81 us
  transfers between devices with their start and end apart: 4, of which 4 were waited for; matrix products, arithmetic and copies ran while one was open for 1% of the time, Pallas kernels for 0%

commit v1 on v0

v1 whole, which is shorter than its diff:
```python
import jax
import jax.numpy as jnp
from jax import lax
from jax.experimental import pallas as pl
from jax.experimental.pallas import tpu as pltpu
from jax.sharding import PartitionSpec as P

LATENT = 512
ROPE = 64
NOPE = 128
VDIM = 128
QRANK = 1536
NY, NZ = 4, 8
MESH = pl.DeviceIdType.MESH
BF16 = jnp.bfloat16
F32 = jnp.float32


def dot(a, b):
    return jnp.dot(a, b, preferred_element_type=F32)


def place():
    ctx = lax.axis_index("ctx")
    head = lax.axis_index("head")
    return ctx // 4, (ctx // 2) % 2, ctx % 2, head // NZ, head % NZ


def ctx_of(x, zh, core):
    return x * 4 + zh * 2 + core


def send(src, dst, send_sem, recv_sem, ctx, head):
    copy = pltpu.make_async_remote_copy(
        src_ref=src,
        dst_ref=dst,
        send_sem=send_sem,
        recv_sem=recv_sem,
        device_id=(ctx, head),
        device_id_type=MESH,
    )
    copy.start()
    return copy


def greet(partners):
    barrier = pltpu.get_barrier_semaphore()
    for ctx, head in partners:
        pl.semaphore_signal(barrier, inc=1, device_id=(ctx, head), device_id_type=MESH)
    pl.semaphore_wait(barrier, len(partners))


def rows(start, size):
    return pl.ds(pl.multiple_of(start, size), size)


def low_kernel(
    hidden_ref,
    qd_ref,
    ld_ref,
    qg_ref,
    lg_ref,
    cos_ref,
    sin_ref,
    q_ref,
    k_ref,
    y_out,
    y_in,
    own_ref,
    z_out,
    z_in,
    sq_out,
    sq_in,
    kz_ref,
    y_s,
    y_r,
    z_s,
    z_r,
    sq_s,
    sq_r,
    qz_s,
    qz_r,
    qy_s,
    qy_r,
    kz_s,
    kz_r,
    ky_s,
    ky_r,
    kx_s,
    kx_r,
    kc_s,
    kc_r,
):
    x, zh, core, y, z = place()
    ctx, head = ctx_of(x, zh, core), y * NZ + z
    ys = [lax.rem(y + d, NY) for d in range(NY)]
    zs = [lax.rem(z + d, NZ) for d in range(NZ)]
    xs = [lax.rem(x + d, 4) for d in range(4)]
    other = 1 - zh
    far = ctx_of(x, other, core)
    partners = [(ctx, ys[d] * NZ + z) for d in range(1, NY)]
    partners += [(ctx, y * NZ + zs[d]) for d in range(1, NZ)]
    partners += [(far, y * NZ + zs[d]) for d in range(NZ)]
    partners += [(ctx_of(xs[d], zh, core), head) for d in range(1, 4)]
    partners += [(ctx_of(x, zh, 1 - core), head)]
    greet(partners)

    hid = hidden_ref[...]
    rot = dot(hid, ld_ref[:, LATENT:])
    rot = jnp.concatenate([rot, jnp.zeros_like(rot)], axis=1)
    waits = []
    for d in (2, 1, 3, 0):
        part = [
            dot(hid, qd_ref[:, rows(ys[d] * 384, 384)]),
            dot(hid, ld_ref[:, rows(ys[d] * 128, 128)]),
            rot,
        ]
        if d:
            for at, piece in zip((0, 384, 512), part):
                y_out[d - 1, :, at : at + piece.shape[1]] = piece.astype(BF16)
            waits.append(
                send(y_out.at[d - 1], y_in.at[d - 1], y_s.at[d - 1], y_r.at[d - 1], ctx, ys[d] * NZ + z)
            )
        else:
            for at, piece in zip((0, 384, 512), part):
                own_ref[:, at : at + piece.shape[1]] = piece
    for copy in waits:
        copy.wait()
    total = own_ref[...]
    for d in range(3):
        total = total + y_in[d].astype(F32)
    own_ref[...] = total
    for i in range(NZ):
        z_out[i] = total[16 * i : 16 * i + 16].astype(BF16)
    waits = []
    for d in (4, 5, 3, 6, 2, 7, 1):
        waits.append(
            send(z_out.at[zs[d]], z_in.at[d - 1], z_s.at[d - 1], z_r.at[d - 1], ctx, y * NZ + zs[d])
        )
    for copy in waits:
        copy.wait()
    mine = own_ref[rows(z * 16, 16), :]
    for d in range(NZ - 1):
        mine = mine + z_in[d].astype(F32)
    q_low, lat, rot = mine[:, :384], mine[:, 384:512], mine[:, 512:]

    lane = lax.broadcasted_iota(jnp.int32, (16, 128), 1)
    q_sq = jnp.sum(q_low * q_low, axis=1, keepdims=True)
    l_sq = jnp.sum(lat * lat, axis=1, keepdims=True)
    sq_out[...] = jnp.where(lane < 64, q_sq, l_sq)
    waits = []
    for d in range(1, NY):
        waits.append(
            send(sq_out, sq_in.at[d - 1], sq_s.at[d - 1], sq_r.at[d - 1], ctx, ys[d] * NZ + z)
        )
    half = ROPE // 2
    here = rows(z * 16, 16)
    swapped = jnp.concatenate([rot[:, half:ROPE], rot[:, :half]], axis=1)
    turned = rot[:, :ROPE] * cos_ref[here, :] + swapped * sin_ref[here, :]
    turned = jnp.concatenate([turned, jnp.zeros_like(turned)], axis=1)
    for copy in waits:
        copy.wait()
    total = sq_out[...] + sq_in[0] + sq_in[1] + sq_in[2]
    q_scale = lax.rsqrt(total[:, 0:1] / QRANK + 1e-06)
    l_scale = lax.rsqrt(total[:, 64:65] / LATENT + 1e-06)
    q_cols = rows(y * 384, 384)
    l_cols = rows(y * 128, 128)
    kz_ref[zh, here, 0:128] = (lat * l_scale * lg_ref[:, l_cols]).astype(BF16)
    kz_ref[zh, here, 128:256] = turned.astype(BF16)
    q_ref[here, q_cols] = (q_low * q_scale * qg_ref[:, q_cols]).astype(BF16)

    kz, qz = [], []
    mine = kz_ref.at[zh, here]
    for d in (4, 5, 3, 6, 2, 7, 1):
        kz.append(send(mine, mine, kz_s.at[d], kz_r.at[d], ctx, y * NZ + zs[d]))
    for d in range(NZ):
        kz.append(send(mine, mine, kz_s.at[NZ + d], kz_r.at[NZ + d], far, y * NZ + zs[d]))
    mine = q_ref.at[here, q_cols]
    for d in (4, 5, 3, 6, 2, 7, 1):
        qz.append(send(mine, mine, qz_s.at[d], qz_r.at[d], ctx, y * NZ + zs[d]))
    for copy in kz:
        copy.wait()
    blocks = [rows(ctx_of(x, i, core) * 128, 128) for i in range(2)]
    ky, kc = [], []
    for i in range(2):
        k_ref[blocks[i], l_cols] = kz_ref[i, :, 0:128]
        k_ref[blocks[i], LATENT:640] = kz_ref[i, :, 128:256]
        mine = k_ref.at[blocks[i], l_cols]
        for d in (2, 1, 3):
            ky.append(send(mine, mine, ky_s.at[i, d], ky_r.at[i, d], ctx, ys[d] * NZ + z))
    for copy in ky:
        copy.wait()
    kx = [[], [], [], []]
    across = ctx_of(x, zh, 1 - core)
    for i in range(2):
        mine = k_ref.at[blocks[i], :]
        for d in (2, 1, 3):
            kx[d].append(
                send(mine, mine, kx_s.at[i, d], kx_r.at[i, d], ctx_of(xs[d], zh, core), head)
            )
        kc.append(send(mine, mine, kc_s.at[i, 0], kc_r.at[i, 0], across, head))
    for copy in qz:
        copy.wait()
    qy = []
    mine = q_ref.at[:, q_cols]
    for d in (2, 1, 3):
        qy.append(send(mine, mine, qy_s.at[d], qy_r.at[d], ctx, ys[d] * NZ + z))
    for d in (1, 3, 2):
        for i in range(2):
            kx[d][i].wait()
            block = rows(ctx_of(lax.rem(x + 4 - d, 4), i, core) * 128, 128)
            mine = k_ref.at[block, :]
            kc.append(send(mine, mine, kc_s.at[i, d], kc_r.at[i, d], across, head))
    for copy in qy + kc:
        copy.wait()


def low_call(hidden, query_down, latent_down, query_gain, latent_gain, cosine, sine):
    dma = pltpu.SemaphoreType.DMA
    vmem = pl.BlockSpec(memory_space=pltpu.VMEM)
    scratch = [
        pltpu.VMEM((3, 128, 640), BF16),
        pltpu.VMEM((3, 128, 640), BF16),
        pltpu.VMEM((128, 640), F32),
        pltpu.VMEM((8, 16, 640), BF16),
        pltpu.VMEM((7, 16, 640), BF16),
        pltpu.VMEM((16, 128), F32),
        pltpu.VMEM((3, 16, 128), F32),
        pltpu.VMEM((2, 128, 256), BF16),
    ]
    for shape in [(3,), (7,), (3,), (8,), (4,), (16,), (2, 4), (2, 4), (2, 4)]:
        scratch += [dma(shape), dma(shape)]
    return pl.pallas_call(
        low_kernel,
        out_shape=(
            jax.ShapeDtypeStruct((128, QRANK), BF16),
            jax.ShapeDtypeStruct((2048, 640), BF16),
        ),
        in_specs=[vmem] * 7,
        out_specs=(vmem, vmem),
        scratch_shapes=scratch,
        compiler_params=pltpu.CompilerParams(
            collective_id=0, has_side_effects=True, vmem_limit_bytes=32 * 1024 * 1024
        ),
        name="low_rank",
    )(hidden, query_down, latent_down, query_gain, latent_gain, cosine, sine)


def out_kernel(
    ho_ref,
    w_ref,
    out_ref,
    g_ref,
    y_out,
    y_in,
    own_ref,
    z_out,
    z_in,
    h_s,
    h_r,
    x_s,
    x_r,
    c_s,
    c_r,
    y_s,
    y_r,
    z_s,
    z_r,
):
    x, zh, core, y, z = place()
    ctx, head = ctx_of(x, zh, core), y * NZ + z
    ys = [lax.rem(y + d, NY) for d in range(NY)]
    zs = [lax.rem(z + d, NZ) for d in range(NZ)]
    xs = [lax.rem(x + d, 4) for d in range(4)]
    other = 1 - zh
    far = ctx_of(x, other, core)
    across = ctx_of(x, zh, 1 - core)
    partners = [(ctx, ys[d] * NZ + z) for d in range(1, NY)]
    partners += [(ctx, y * NZ + zs[d]) for d in range(1, NZ)]
    partners += [(ctx_of(xs[d], zh, core), head) for d in range(1, 4)]
    partners += [(far, head), (across, head)]
    greet(partners)

    def block(d, half):
        return g_ref.at[rows(ctx_of(lax.rem(x + 4 - d, 4), half, core) * 128, 128), :]

    g_ref[rows(ctx * 128, 128), :] = ho_ref[...]
    mine = block(0, zh)
    over = send(mine, mine, h_s, h_r, far, head)
    kx, kc = {}, []
    for half, first in ((zh, 0), (other, 1)):
        if first:
            over.wait()
        mine = block(0, half)
        for d in (2, 1, 3):
            kx[first, d] = send(
                mine, mine, x_s.at[first, d], x_r.at[first, d], ctx_of(xs[d], zh, core), head
            )
        kc.append(send(mine, mine, c_s.at[first, 0], c_r.at[first, 0], across, head))
    for half, first in ((zh, 0), (other, 1)):
        for d in (1, 3, 2):
            kx[first, d].wait()
            mine = block(d, half)
            kc.append(send(mine, mine, c_s.at[first, d], c_r.at[first, d], across, head))
    for copy in kc:
        copy.wait()

    w = w_ref[...]
    waits = []
    for d in (2, 1, 3, 0):

        @pl.loop(0, 4)
        def _(i):
            at = rows(i * 128, 128)
            part = dot(g_ref[rows(ys[d] * 512 + i * 128, 128), :], w)
            if d:
                y_out[d - 1, at, :] = part.astype(BF16)
            else:
                own_ref[at, :] = part

        if d:
            waits.append(
                send(y_out.at[d - 1], y_in.at[d - 1], y_s.at[d - 1], y_r.at[d - 1], ctx, ys[d] * NZ + z)
            )
    for copy in waits:
        copy.wait()

    @pl.loop(0, NZ)
    def _(i):
        at = rows(i * 64, 64)
        total = own_ref[at, :]
        for d in range(3):
            total = total + y_in[d, at, :].astype(F32)
        own_ref[at, :] = total
        z_out[i] = total.astype(BF16)

    waits = []
    for d in (4, 5, 3, 6, 2, 7, 1):
        waits.append(
            send(z_out.at[zs[d]], z_in.at[d - 1], z_s.at[d - 1], z_r.at[d - 1], ctx, y * NZ + zs[d])
        )
    for copy in waits:
        copy.wait()
    total = own_ref[rows(z * 64, 64), :]
    for d in range(NZ - 1):
        total = total + z_in[d].astype(F32)
    out_ref[...] = total.astype(BF16)


def out_call(head_out, out_proj):
    dma = pltpu.SemaphoreType.DMA
    vmem = pl.BlockSpec(memory_space=pltpu.VMEM)
    cols = out_proj.shape[1]
    scratch = [
        pltpu.VMEM((2048, 512), BF16),
        pltpu.VMEM((3, 512, cols), BF16),
        pltpu.VMEM((3, 512, cols), BF16),
        pltpu.VMEM((512, cols), F32),
        pltpu.VMEM((8, 64, cols), BF16),
        pltpu.VMEM((7, 64, cols), BF16),
        dma,
        dma,
    ]
    for shape in [(2, 4), (2, 4), (3,), (7,)]:
        scratch += [dma(shape), dma(shape)]
    return pl.pallas_call(
        out_kernel,
        out_shape=jax.ShapeDtypeStruct((64, cols), BF16),
        in_specs=[vmem] * 2,
        out_specs=vmem,
        scratch_shapes=scratch,
        compiler_params=pltpu.CompilerParams(
            collective_id=1, has_side_effects=True, vmem_limit_bytes=32 * 1024 * 1024
        ),
        name="out_sum",
    )(head_out, out_proj)


def body(
    hidden,
    query_down,
    latent_down,
    query_gain,
    latent_gain,
    query_up,
    key_absorb,
    value_absorb,
    out_proj,
    doc_start,
    positions,
):
    tok_rows = hidden.shape[0]
    heads_here = query_up.shape[1] // (NOPE + ROPE)
    half = ROPE // 2
    freqs = 10000.0 ** (-2.0 * jnp.arange(half, dtype=F32) / ROPE)
    angles = positions.astype(F32)[:, None] * freqs[None, :]
    cosine, sine = jnp.cos(angles), jnp.sin(angles)
    cosine = jnp.concatenate([cosine, cosine], axis=1)
    sine = jnp.concatenate([-sine, sine], axis=1)
    query_normed, keys = low_call(
        hidden, query_down, latent_down, query_gain[None, :], latent_gain[None, :], cosine, sine
    )
    keys = keys[:, : LATENT + ROPE]
    query_full = dot(query_normed, query_up).reshape(tok_rows, heads_here, NOPE + ROPE)
    query_nope = query_full[:, :, :NOPE].astype(BF16)
    raw = query_full[:, :, NOPE:]
    swapped = jnp.concatenate([raw[..., half:], raw[..., :half]], axis=-1)
    query_rot = (raw * cosine[:, None, :] + swapped * sine[:, None, :]).astype(BF16)
    query_lat = jnp.einsum(
        "thn,lhn->thl",
        query_nope,
        key_absorb.reshape(LATENT, heads_here, NOPE),
        preferred_element_type=F32,
    ).astype(BF16)
    queries = jnp.concatenate([query_lat, query_rot], axis=2).reshape(
        tok_rows * heads_here, LATENT + ROPE
    )
    first_row = lax.axis_index("ctx") * tok_rows
    query_index = jnp.repeat(first_row + jnp.arange(tok_rows, dtype=jnp.int32), heads_here)
    query_doc = jnp.repeat(doc_start, heads_here)
    scale = (NOPE + ROPE) ** (-0.5)
    key_index = jnp.arange(keys.shape[0], dtype=jnp.int32)
    scores = (
        lax.dot_general(queries, keys, (((1,), (1,)), ((), ())), preferred_element_type=F32) * scale
    )
    visible = (key_index[None, :] <= query_index[:, None]) & (
        key_index[None, :] >= query_doc[:, None]
    )
    scores = jnp.where(visible, scores, -1e30)
    top = jnp.max(scores, axis=1)
    expo = jnp.where(visible, jnp.exp(scores - top[:, None]), 0.0)
    total = jnp.sum(expo, axis=1)
    weighted = dot(expo.astype(BF16), keys[:, :LATENT])
    mixed = (weighted / total[:, None]).astype(BF16).reshape(tok_rows, heads_here, LATENT)
    head_out = jnp.einsum(
        "thl,lhv->thv",
        mixed,
        value_absorb.reshape(LATENT, heads_here, VDIM),
        preferred_element_type=F32,
    ).astype(BF16)
    return out_call(head_out.reshape(tok_rows, heads_here * VDIM), out_proj)


def solution(mesh):
    in_specs = (
        P("ctx", "head"),
        P("head", None),
        P("head", None),
        P(),
        P(),
        P(None, "head"),
        P(None, "head"),
        P(None, "head"),
        P("head", "ctx"),
        P("ctx"),
        P("ctx"),
    )
    out_specs = P("head", "ctx")
    return jax.shard_map(body, mesh=mesh, in_specs=in_specs, out_specs=out_specs, check_vma=False)
```

time: 915 us -> 175 us (0.19)
  the two profiles are of different devices: /device:TPU:2 before, /device:TPU:1 now
where the time goes in v1:
time: 175 us; the launch traced here: 174 us
  Pallas kernels  148 us (85%)
  local copies, waits for them, and re-layouts  11.1 us (6%)
  matrix products  10.6 us (6%)
  other arithmetic  4.68 us (3%)
    pallas_call x1, Pallas kernels, out_call(): pl.pallas_call(out_kernel, out_shape=jax.ShapeDtypeStruct((64, cols), BF1...  78.7 us
    pallas_call x1, Pallas kernels, low_call(): pl.pallas_call(low_kernel, out_shape=(jax.ShapeDtypeStruct((128, QRANK),...  69.2 us
    unnamed x22, local copies, waits for them, and re-layouts  7.09 us
    dot_general x1, matrix products, body(): lax.dot_general(queries, keys, (((1,), (1,)), ((), ())), preferred_elemen...  4.38 us

profile of v1, /device:TPU:1, one launch (start us, length us, event | category | flops | bytes accessed | tf_op | source)
XLA Modules:
  0.0 174.4 jit_solution(3029165183446057584)
XLA Ops:
  0.0 0.8 convert_element_type.25
  0.8 0.3 fusion.24
  1.1 0.1 pad_maximum_fusion.1
  1.2 0.9 copy.35.hidden_ref
  2.2 0.7 broadcast_in_dim.29.qg_ref
  2.9 1.1 copy-done.1
  4.0 1.0 copy-done.2
  4.9 0.7 copy-done.3
  5.6 69.2 %low_rank.1 = (bf16[128,1536]{1,0:T(8,128)(2,1)S(1)}, bf16[2048,640]{1,0:T(8,128)(2,1)S(1)}) custom-call(bf16[128,224]{1,0:T(8,128)(2,1)S(1)} %copy.35.hidden_ref, bf16[224,1536]{1,0:T(8,128)(2,1)S(1)} %copy-done.1, bf16[224,576]{1,0:T(8,128)(2,1)S(1)} %copy-done.2, f32[1,1536]{1,0:T(1,128)S(1)} %broadcast_in_dim.29.qg_ref, f32[1,512]{1,0:T(1,128)S(1)} %bitcast.19, ...), custom_call_target="tpu_custom_call" | custom-call | tf_op jit(solution)/shard_map/low_rank/pallas_call | solution.py:233
  74.8 1.0 fusion.29
  75.8 0.5 copy-done.4
  76.3 0.1 copy.52
  76.5 0.1 copy.53
  76.6 0.8 copy.51
  77.5 1.1 fusion.23
  78.5 1.4 fusion.14
  80.0 0.5 copy.42
  80.5 1.2 reshape.32
  81.7 0.1 broadcast_in_dim.27
  81.8 0.1 le.18
  81.9 0.1 broadcast_in_dim.28
  82.0 0.1 ge.6
  82.1 4.4 %fusion.1 = (f32[512]{0:T(512)S(1)}, f32[512,2048]{1,0:T(8,128)S(1)}) fusion(s32[512]{0:T(512)S(1)} %ge.6, s32[512]{0:T(512)S(1)} %le.18, bf16[512,576]{1,0:T(8,128)(2,1)} %reshape.32, bf16[2048,640]{1,0:T(8,128)(2,1)} %copy-done.4), kind=kOutput, calls=%fused_computation.5 | convolution fusion | flops 1214250496 | bytes 7411712 | tf_op jit(solution)/shard_map/dot_general | solution.py:424
  86.5 2.3 %fusion.4 = f32[512]{0:T(512)S(1)} fusion(f32[512,2048]{1,0:T(8,128)S(1)} %get-tuple-element.15, f32[512]{0:T(512)S(1)} %get-tuple-element.14, s32[512]{0:T(512)S(1)} %ge.6, s32[512]{0:T(512)S(1)} %le.18), kind=kLoop, calls=%fused_computation.8 | loop fusion | flops 8388096 | bytes 4202496 | tf_op jit(solution)/shard_map/reduce_sum | solution.py:432
  88.8 2.4 %divide_convert_fusion = bf16[512,512]{1,0:T(8,128)(2,1)S(1)} fusion(bf16[2048,640]{1,0:T(8,128)(2,1)S(1)} %copy-done.5, f32[512,2048]{1,0:T(8,128)S(1)} %get-tuple-element.15, f32[512]{0:T(512)S(1)} %get-tuple-element.14, s32[512]{0:T(512)S(1)} %ge.6, s32[512]{0:T(512)S(1)} %le.18, f32[512]{0:T(512)S(1)} %fusion.4), kind=kOutput, calls=%fused_computation.20 | convolution fusion | flops 1082654720 | bytes 6823936 | tf_op jit(solution)/shard_map/dot_general | solution.py:20
  91.2 0.9 reshape.33
  92.2 0.2 copy.49
  92.4 1.4 convolution_convert_fusion.1
  93.7 0.1 copy.50.ho_ref
  93.9 1.2 copy.46.w_ref
  95.1 78.7 %out_sum.1 = bf16[64,448]{1,0:T(8,128)(2,1)S(1)} custom-call(bf16[128,512]{1,0:T(8,128)(2,1)S(1)} %copy.50.ho_ref, bf16[512,448]{1,0:T(8,128)(2,1)S(1)} %copy.46.w_ref), custom_call_target="tpu_custom_call" | custom-call | tf_op jit(solution)/shard_map/out_sum/pallas_call | solution.py:366
  173.8 0.6 copy.62
  (17 shorter events, 0.1 us)
Async XLA Ops:
  0.0 74.8 %copy-start = (bf16[1536,768]{1,0:T(8,128)(2,1)S(1)}, bf16[1536,768]{1,0:T(8,128)(2,1)}, u32[]{:S(2)}) copy-start(bf16[1536,768]{1,0:T(8,128)(2,1)} %param.16) | copy-start | bytes 7077892
  2.9 1.1 copy-start.1
  4.0 1.0 copy-start.2
  4.9 0.7 copy-start.3
  74.8 1.5 copy-start.4
  76.3 5.6 %copy-start.7 = (s32[128]{0:T(128)S(1)}, s32[128]{0:T(128)}, u32[]{:S(2)}) copy-start(s32[128]{0:T(128)} %param.20) | copy-start | bytes 1540
  86.5 2.3 %copy-start.5 = (bf16[2048,640]{1,0:T(8,128)(2,1)S(1)}, bf16[2048,640]{1,0:T(8,128)(2,1)}, u32[]{:S(2)}) copy-start(bf16[2048,640]{1,0:T(8,128)(2,1)} %copy-done.4) | copy-start | bytes 7864324
  88.8 3.4 %copy-start.6 = (bf16[512,512]{1,0:T(8,128)(2,1)S(1)}, bf16[512,512]{1,0:T(8,128)(2,1)}, u32[]{:S(2)}) copy-start(bf16[512,512]{1,0:T(8,128)(2,1)} %param.18) | copy-start | bytes 1572868

commit v2 on v0

v2 whole, which is shorter than its diff:
```python
import jax
import jax.numpy as jnp
import numpy as np
from jax import lax
from jax.experimental import pallas as pl
from jax.experimental.pallas import tpu as pltpu
from jax.sharding import PartitionSpec as P

LATENT = 512
ROPE = 64
NOPE = 128
VDIM = 128
QRANK = 1536
NX, NY, NZ = 4, 4, 8
KEY = LATENT + 2 * ROPE
SCALE = (NOPE + ROPE) ** (-0.5)
MESH = pl.DeviceIdType.MESH
BF16 = jnp.bfloat16
F32 = jnp.float32
FAR_FIRST = (4, 5, 3, 6, 2, 7, 1)
N_WIRES = 176


def dot(a, b):
    return jnp.dot(a, b, preferred_element_type=F32)


def dot_t(a, b):
    return lax.dot_general(a, b, (((1,), (1,)), ((), ())), preferred_element_type=F32)


def rows(start, size):
    return pl.ds(pl.multiple_of(start, size), size)


def ctx_of(x, zh, core):
    return x * 4 + zh * 2 + core


class Wires:
    def __init__(self, send_sems, recv_sems):
        self.send_sems, self.recv_sems, self.used = send_sems, recv_sems, 0

    def send(self, src, dst, to):
        at = self.used
        self.used += 1
        copy = pltpu.make_async_remote_copy(
            src_ref=src,
            dst_ref=dst,
            send_sem=self.send_sems.at[at],
            recv_sem=self.recv_sems.at[at],
            device_id=to,
            device_id_type=MESH,
        )
        copy.start()
        return copy


def wait_all(copies):
    for copy in copies:
        copy.wait()


def kernel(
    hidden_hbm,
    qd_hbm,
    ld_hbm,
    qg_hbm,
    lg_hbm,
    qup_hbm,
    ka_hbm,
    va_hbm,
    wo_hbm,
    doc_hbm,
    pos_hbm,
    freq_hbm,
    out_ref,
    hidden_ref,
    qd_ref,
    ld_ref,
    qg_ref,
    lg_ref,
    qup_ref,
    ka_ref,
    va_ref,
    wo_ref,
    doc_ref,
    pos_ref,
    freq_ref,
    gain_ref,
    lgain_ref,
    cos_ref,
    sin_ref,
    kv_out,
    kv_in,
    q_out,
    q_in,
    kv_own,
    q_own,
    kvz_out,
    kvz_in,
    qz_out,
    qz_in,
    sq_out,
    sq_in,
    kz_ref,
    q_ref,
    k_ref,
    qc_ref,
    s_ref,
    ho_ref,
    g_ref,
    own_ref,
    z_out,
    z_in,
    fin_out,
    fin_ref,
    load_sems,
    send_sems,
    recv_sems,
):
    ctx = lax.axis_index("ctx")
    head = lax.axis_index("head")
    x, zh, core = ctx // 4, (ctx // 2) % 2, ctx % 2
    y, z = head // NZ, head % NZ
    ys = [lax.rem(y + d, NY) for d in range(NY)]
    zs = [lax.rem(z + d, NZ) for d in range(NZ)]
    other = 1 - zh
    far = ctx_of(x, other, core)
    to_y = [(ctx, ys[d] * NZ + z) for d in range(NY)]
    to_z = [(ctx, y * NZ + zs[d]) for d in range(NZ)]
    to_far = [(far, y * NZ + zs[d]) for d in range(NZ)]
    to_x = [(ctx_of(lax.rem(x + d, NX), zh, core), head) for d in range(NX)]
    to_core = (ctx_of(x, zh, 1 - core), head)
    wires = Wires(send_sems, recv_sems)

    loads = {}
    for i, (name, src, dst) in enumerate(
        [
            ("hidden", hidden_hbm, hidden_ref),
            ("ld", ld_hbm, ld_ref),
            ("qd", qd_hbm, qd_ref),
            ("qg", qg_hbm, qg_ref),
            ("lg", lg_hbm, lg_ref),
            ("pos", pos_hbm, pos_ref),
            ("doc", doc_hbm, doc_ref),
            ("freq", freq_hbm, freq_ref),
            ("qup", qup_hbm, qup_ref),
            ("ka", ka_hbm, ka_ref),
            ("va", va_hbm, va_ref),
            ("wo", wo_hbm, wo_ref.at[y]),
        ]
    ):
        loads[name] = pltpu.make_async_copy(src, dst, load_sems.at[i])
        loads[name].start()
    barrier = pltpu.get_barrier_semaphore()
    partners = to_y[1:] + to_z[1:] + to_far + to_x[1:] + [to_core]
    for to in partners:
        pl.semaphore_signal(barrier, inc=1, device_id=to, device_id_type=MESH)
    pl.semaphore_wait(barrier, len(partners))

    loads["hidden"].wait()
    loads["ld"].wait()
    hid = hidden_ref[...]
    rot = dot(hid, ld_ref[:, LATENT:])
    rot = jnp.concatenate([rot, jnp.zeros_like(rot)], axis=1)
    kv_y = []
    for d in (2, 1, 3):
        kv_out[d - 1, :, 0:128] = dot(hid, ld_ref[:, rows(ys[d] * 128, 128)]).astype(BF16)
        kv_out[d - 1, :, 128:256] = rot.astype(BF16)
        kv_y.append(wires.send(kv_out.at[d - 1], kv_in.at[d - 1], to_y[d]))
    l_cols = rows(y * 128, 128)
    q_cols = rows(y * 384, 384)
    kv_own[:, 0:128] = dot(hid, ld_ref[:, l_cols])
    kv_own[:, 128:256] = rot
    loads["qd"].wait()
    q_y = []
    for d in (2, 1, 3):
        q_out[d - 1] = dot(hid, qd_ref[:, rows(ys[d] * 384, 384)]).astype(BF16)
        q_y.append(wires.send(q_out.at[d - 1], q_in.at[d - 1], to_y[d]))
    q_own[...] = dot(hid, qd_ref[:, q_cols])

    loads["pos"].wait()
    loads["freq"].wait()
    angles = freq_ref[...] * pos_ref[...].astype(F32)[None, :]
    cosine, sine = jnp.cos(angles), jnp.sin(angles)
    cos_ref[...] = jnp.concatenate([cosine, cosine, cosine, cosine], axis=0).T
    sin_ref[...] = jnp.concatenate([-sine, sine, -sine, sine], axis=0).T
    loads["qg"].wait()
    loads["lg"].wait()
    gain_ref[...] = qg_ref[...][None, :]
    lgain_ref[...] = lg_ref[...][None, :]

    def over_y(copies, own, received):
        wait_all(copies)
        total = own[...]
        for d in range(NY - 1):
            total = total + received[d].astype(F32)
        own[...] = total
        return total

    def to_all_z(total, out, received):
        for i in range(NZ):
            out[i] = total[16 * i : 16 * i + 16].astype(BF16)
        return [wires.send(out.at[zs[d]], received.at[d - 1], to_z[d]) for d in FAR_FIRST]

    here = rows(z * 16, 16)

    def over_z(copies, own, received):
        wait_all(copies)
        total = own[here, :]
        for d in range(NZ - 1):
            total = total + received[d].astype(F32)
        return total

    def square(i, values):
        total = jnp.sum(values * values, axis=1, keepdims=True)
        sq_out[i] = jnp.broadcast_to(total, (16, 128))
        return [wires.send(sq_out.at[i], sq_in.at[i, d - 1], to_y[d]) for d in (2, 1, 3)]

    def scale_of(i, copies, count):
        wait_all(copies)
        total = sq_out[i] + sq_in[i, 0] + sq_in[i, 1] + sq_in[i, 2]
        return lax.rsqrt(total[:, 0:1] / count + 1e-06)

    kv_z = to_all_z(over_y(kv_y, kv_own, kv_in), kvz_out, kvz_in)
    q_z = to_all_z(over_y(q_y, q_own, q_in), qz_out, qz_in)
    mine = over_z(kv_z, kv_own, kvz_in)
    lat, rot = mine[:, :128], mine[:, 128:]
    kv_sq = square(0, lat)
    half = ROPE // 2
    swapped = jnp.concatenate([rot[:, half:ROPE], rot[:, :half]], axis=1)
    turned = rot[:, :ROPE] * cos_ref[here, :ROPE] + swapped * sin_ref[here, :ROPE]
    kz_ref[zh, here, 128:256] = jnp.concatenate([turned, jnp.zeros_like(turned)], axis=1).astype(BF16)
    q_low = over_z(q_z, q_own, qz_in)
    q_sq = square(1, q_low)

    l_scale = scale_of(0, kv_sq, LATENT)
    kz_ref[zh, here, 0:128] = (lat * l_scale * lgain_ref[:, l_cols]).astype(BF16)
    piece = kz_ref.at[zh, here]
    kz = [wires.send(piece, piece, to_z[d]) for d in FAR_FIRST]
    kz += [wires.send(piece, piece, to_far[d]) for d in range(NZ)]
    q_scale = scale_of(1, q_sq, QRANK)
    q_ref[here, q_cols] = (q_low * q_scale * gain_ref[:, q_cols]).astype(BF16)
    piece = q_ref.at[here, q_cols]
    qz = [wires.send(piece, piece, to_z[d]) for d in FAR_FIRST]

    def key_rows(d, i):
        return rows(ctx_of(lax.rem(x + NX - d, NX), i, core) * 128, 128)

    wait_all(kz)
    for i in range(2):
        k_ref[key_rows(0, i), l_cols] = kz_ref[i, :, 0:128]
        k_ref[key_rows(0, i), LATENT:KEY] = kz_ref[i, :, 128:256]

    def key_over_y(d, i):
        piece = k_ref.at[key_rows(d, i), l_cols]
        return [wires.send(piece, piece, to_y[e]) for e in (2, 1, 3)]

    first_y = key_over_y(0, 0)
    second_x, second_y = {}, {}
    for d in (2, 1, 3):
        second_x[d] = []
        for cols in (l_cols, pl.ds(LATENT, 128)):
            piece = k_ref.at[key_rows(0, 1), cols]
            second_x[d].append(wires.send(piece, piece, to_x[d]))
    second_y[0] = key_over_y(0, 1)
    wait_all(qz)
    piece = q_ref.at[:, q_cols]
    q_all = [wires.send(piece, piece, to_y[d]) for d in (2, 1, 3)]
    wait_all(first_y)
    first_x = {}
    for d in (2, 1, 3):
        piece = k_ref.at[key_rows(0, 0), :]
        first_x[d] = [wires.send(piece, piece, to_x[d])]
    for d in (1, 3, 2):
        wait_all(second_x[d])
        second_y[d] = key_over_y(d, 1)
    loads["wo"].wait()
    weights = [wires.send(wo_ref.at[y], wo_ref.at[y], to_y[d]) for d in (2, 1, 3)]

    key_core = {}

    def key_to_core(d):
        if d:
            wait_all(first_x[d])
        wait_all(second_y[d])
        key_core[d] = []
        for i in range(2):
            piece = k_ref.at[key_rows(d, i), :]
            key_core[d].append(wires.send(piece, piece, to_core))

    for name in ("qup", "ka", "va", "doc"):
        loads[name].wait()
    wait_all(q_all)
    key_to_core(0)
    full = dot(q_ref[...], qup_ref[...])
    cosine, sine = cos_ref[:, :ROPE], sin_ref[:, :ROPE]
    for h in range(4):
        at = h * (NOPE + ROPE)
        nope = full[:, at : at + NOPE].astype(BF16)
        raw = full[:, at + NOPE : at + NOPE + ROPE]
        swapped = jnp.concatenate([raw[:, half:], raw[:, :half]], axis=1)
        turned = raw * cosine + swapped * sine
        low = dot_t(nope, ka_ref[:, h * NOPE : (h + 1) * NOPE])
        mine = slice(h * 128, h * 128 + 128)
        qc_ref[mine, :LATENT] = low.astype(BF16)
        qc_ref[mine, LATENT:] = jnp.concatenate([turned, jnp.zeros_like(turned)], axis=1).astype(BF16)

    doc = jnp.broadcast_to(doc_ref[...].astype(F32)[None, :], (128, 128)).T[:, 0:1].astype(jnp.int32)
    query_index = ctx * 128 + lax.broadcasted_iota(jnp.int32, (128, 512), 0)
    key_lane = lax.broadcasted_iota(jnp.int32, (128, 512), 1)
    top = [None] * 4

    def scores(d):
        wait_all(key_core[d])
        at = rows(lax.rem(x + NX - d, NX) * 512, 512)
        key_index = key_lane + lax.rem(x + NX - d, NX) * 512
        bias = jnp.where((key_index <= query_index) & (key_index >= doc), 0.0, -1e30)
        block = dot_t(qc_ref[...], k_ref[at, :])
        for h in range(4):
            mine = slice(h * 128, h * 128 + 128)
            values = block[mine] * SCALE + bias
            s_ref[mine, at] = values
            most = jnp.max(values, axis=1, keepdims=True)
            top[h] = most if top[h] is None else jnp.maximum(top[h], most)

    key_to_core(1)
    scores(0)
    key_to_core(3)
    scores(1)
    key_to_core(2)
    scores(3)
    scores(2)

    here_zc, far_zc = zh * 2 + core, other * 2 + core
    cols = rows(y * 256, 256)

    def mix(pair):
        mine = slice(pair * 256, pair * 256 + 256)
        most = jnp.concatenate([top[2 * pair], top[2 * pair + 1]], axis=0)
        weighted = jnp.zeros((256, LATENT), F32)
        total = jnp.zeros((256, 1), F32)
        for j in range(4):
            expo = jnp.exp(s_ref[mine, 512 * j : 512 * j + 512] - most)
            total = total + jnp.sum(expo, axis=1, keepdims=True)
            weighted = weighted + dot(expo.astype(BF16), k_ref[512 * j : 512 * j + 512, :LATENT])
        mixed = (weighted / total).astype(BF16)
        for i in range(2):
            at = (2 * pair + i) * VDIM
            result = dot(mixed[128 * i : 128 * i + 128], va_ref[:, at : at + VDIM]).astype(BF16)
            for part in range(4):
                for side in range(2):
                    first = 64 * side + 16 * part
                    ho_ref[pair, part, side, :, 128 * i : 128 * i + 128] = result[first : first + 16]
        g_ref[pair, here_zc, :, x, :, cols] = ho_ref[pair, y]
        spot = g_ref.at[pair, here_zc, :, x, :, cols]
        return [wires.send(ho_ref.at[pair, ys[d]], spot, to_y[d]) for d in (2, 1, 3)]

    def block(pair, zc, d):
        return g_ref.at[pair, zc, :, lax.rem(x + NX - d, NX)]

    def spread(pair, zc, over_x):
        piece = block(pair, zc, 0)
        for d in (2, 1, 3):
            over_x[pair, zc is far_zc, d] = wires.send(piece, piece, to_x[d])
        return wires.send(piece, piece, to_core)

    over_x, over_core, over_far = {}, [], {}

    def launch(pair, copies):
        wait_all(copies)
        piece = block(pair, here_zc, 0)
        over_far[pair] = wires.send(piece, piece, to_far[0])
        over_core.append(spread(pair, here_zc, over_x))

    handed = mix(0)
    second = mix(1)
    launch(0, handed)
    launch(1, second)
    for pair in range(2):
        over_far[pair].wait()
        over_core.append(spread(pair, far_zc, over_x))
    for pair in range(2):
        for zc in (here_zc, far_zc):
            for d in (1, 3, 2):
                over_x[pair, zc is far_zc, d].wait()
                piece = block(pair, zc, d)
                over_core.append(wires.send(piece, piece, to_core))
    wait_all(over_core)
    wait_all(weights)

    pair_at, odd = z // 2, z % 2
    sums = {}
    for k in (2, 1, 3, 0):
        zc = lax.rem(pair_at + k, 4)
        total = jnp.zeros((128, out_ref.shape[1]), F32)
        for pair in range(2):
            tokens = g_ref[pair, zc].reshape(128, 1024)
            for i in range(NY):
                total = total + dot(
                    tokens[:, 256 * i : 256 * i + 256], wo_ref[i, 256 * pair : 256 * pair + 256, :]
                )
        for side in range(2):
            part = total[64 * side : 64 * side + 64]
            part = jnp.concatenate([part[:32], part[32:]], axis=1)
            z_out[k, side] = part.astype(BF16)
            if k == 0:
                own_ref[side] = part
        for flip in (0, 1):
            if k or flip:
                side = odd + flip - 2 * odd * flip
                to = (ctx, y * NZ + zc * 2 + side)
                sums[k, flip] = wires.send(z_out.at[k, side], z_in.at[k, flip], to)
    total = own_ref[odd]
    for key in ((0, 1), (1, 0), (1, 1), (3, 0), (3, 1), (2, 0), (2, 1)):
        sums[key].wait()
        total = total + z_in[key].astype(F32)
    width = out_ref.shape[1]
    result = jnp.concatenate([total[:, :width], total[:, width:]], axis=0).astype(BF16)
    for i in range(NX):
        fin_out[i] = result[16 * i : 16 * i + 16]
    fin_ref[y] = fin_out[y]
    wait_all([wires.send(fin_out.at[ys[d]], fin_ref.at[y], to_y[d]) for d in (2, 1, 3)])
    for i in range(NY):
        out_ref[16 * i : 16 * i + 16, :] = fin_ref[i]
    assert wires.used <= N_WIRES


def body(
    hidden,
    query_down,
    latent_down,
    query_gain,
    latent_gain,
    query_up,
    key_absorb,
    value_absorb,
    out_proj,
    doc_start,
    positions,
):
    half = ROPE // 2
    freqs = 10000.0 ** (-2.0 * np.arange(half) / ROPE)
    freqs = np.broadcast_to(freqs.astype(np.float32)[:, None], (half, 128))
    width = out_proj.shape[1]
    vmem = pltpu.VMEM
    operands = (
        hidden,
        query_down,
        latent_down,
        query_gain,
        latent_gain,
        query_up,
        key_absorb,
        value_absorb,
        out_proj,
        doc_start,
        positions,
        jnp.asarray(freqs),
    )
    scratch = [vmem(a.shape, a.dtype) for a in operands]
    scratch[8] = vmem((NY,) + out_proj.shape, BF16)
    scratch += [
        vmem((1, QRANK), F32),
        vmem((1, LATENT), F32),
        vmem((128, 128), F32),
        vmem((128, 128), F32),
        vmem((3, 128, 256), BF16),
        vmem((3, 128, 256), BF16),
        vmem((3, 128, 384), BF16),
        vmem((3, 128, 384), BF16),
        vmem((128, 256), F32),
        vmem((128, 384), F32),
        vmem((8, 16, 256), BF16),
        vmem((7, 16, 256), BF16),
        vmem((8, 16, 384), BF16),
        vmem((7, 16, 384), BF16),
        vmem((2, 16, 128), F32),
        vmem((2, 3, 16, 128), F32),
        vmem((2, 128, 256), BF16),
        vmem((128, QRANK), BF16),
        vmem((2048, KEY), BF16),
        vmem((512, KEY), BF16),
        vmem((512, 2048), F32),
        vmem((2, 4, 2, 16, 256), BF16),
        vmem((2, 4, 2, 4, 16, 1024), BF16),
        vmem((2, 32, 2 * width), F32),
        vmem((4, 2, 32, 2 * width), BF16),
        vmem((4, 2, 32, 2 * width), BF16),
        vmem((4, 16, width), BF16),
        vmem((4, 16, width), BF16),
        pltpu.SemaphoreType.DMA((len(operands),)),
        pltpu.SemaphoreType.DMA((N_WIRES,)),
        pltpu.SemaphoreType.DMA((N_WIRES,)),
    ]
    return pl.pallas_call(
        kernel,
        out_shape=jax.ShapeDtypeStruct((64, width), BF16),
        in_specs=[pl.BlockSpec(memory_space=pl.ANY)] * len(operands),
        out_specs=pl.BlockSpec(memory_space=pltpu.VMEM),
        scratch_shapes=scratch,
        compiler_params=pltpu.CompilerParams(
            collective_id=0, has_side_effects=True, vmem_limit_bytes=48 * 1024 * 1024
        ),
        name="latent_attention",
    )(*operands)


def solution(mesh):
    in_specs = (
        P("ctx", "head"),
        P("head", None),
        P("head", None),
        P(),
        P(),
        P(None, "head"),
        P(None, "head"),
        P(None, "head"),
        P("head", "ctx"),
        P("ctx"),
        P("ctx"),
    )
    out_specs = P("head", "ctx")
    return jax.shard_map(body, mesh=mesh, in_specs=in_specs, out_specs=out_specs, check_vma=False)
```

time: 915 us -> 139 us (0.15)
  the two profiles are of different devices: /device:TPU:2 before, /device:TPU:1 now
where the time goes in v2:
time: 139 us; the launch traced here: 138 us
  Pallas kernels  126 us (91%)
  local copies, waits for them, and re-layouts  12 us (9%)
    pallas_call x1, Pallas kernels, body(): pl.pallas_call(kernel, out_shape=jax.ShapeDtypeStruct((64, width), BF16),...  126 us
    unnamed x21, local copies, waits for them, and re-layouts  11.3 us

profile of v2, /device:TPU:1, one launch (start us, length us, event | category | flops | bytes accessed | tf_op | source)
XLA Modules:
  0.0 138.5 jit_solution(655777964657274494)
XLA Ops:
  0.0 0.9 copy.13.hidden_hbm
  0.9 1.2 copy.14.wo_hbm
  2.2 0.7 jit_solution_.3.freq_hbm
  2.9 0.0 copy-start
  2.9 1.7 %copy-done = bf16[1536,768]{1,0:T(8,128)(2,1)S(1)} copy-done((bf16[1536,768]{1,0:T(8,128)(2,1)S(1)}, bf16[1536,768]{1,0:T(8,128)(2,1)}, u32[]{:S(2)}) %copy-start) | copy-done | bytes 2359320
  4.5 0.0 copy-start.1
  4.6 1.1 copy-done.1
  5.6 0.0 copy-start.2
  5.7 1.0 copy-done.2
  6.7 0.0 copy-start.3
  6.7 1.0 copy-done.3
  7.7 0.0 copy-start.4
  7.7 1.0 copy-done.4
  8.7 0.0 copy-start.5
  8.7 0.7 copy-done.5
  9.4 0.0 copy-start.6
  9.4 0.7 copy-done.6
  10.1 0.0 copy-start.7
  10.1 0.7 copy-done.7
  10.7 0.0 copy-start.8
  10.7 0.7 copy-done.8
  11.4 126.4 %latent_attention.1 = bf16[64,448]{1,0:T(8,128)(2,1)S(1)} custom-call(bf16[128,224]{1,0:T(8,128)(2,1)S(1)} %copy.13.hidden_hbm, bf16[224,1536]{1,0:T(8,128)(2,1)S(1)} %copy-done.1, bf16[224,576]{1,0:T(8,128)(2,1)S(1)} %copy-done.4, f32[1536]{0:T(1024)S(1)} %copy-done.5, f32[512]{0:T(512)S(1)} %copy-done.6, bf16[1536,768]{1,0:T(8,128)(2,1)S(1)} %copy-done, ...), custom_call_target="tpu_custom_call" | custom-call | tf_op jit(solution)/shard_map/latent_attention/pallas_call | solution.py:497
  137.8 0.6 copy.16
Async XLA Ops:
  2.9 1.7 %copy-start = (bf16[1536,768]{1,0:T(8,128)(2,1)S(1)}, bf16[1536,768]{1,0:T(8,128)(2,1)}, u32[]{:S(2)}) copy-start(bf16[1536,768]{1,0:T(8,128)(2,1)} %qup_hbm.1) | copy-start | bytes 7077892
  4.5 1.1 copy-start.1
  5.6 1.0 copy-start.2
  6.7 1.0 copy-start.3
  7.7 1.0 copy-start.4
  8.7 0.7 copy-start.5
  9.4 0.7 copy-start.6
  10.1 0.7 copy-start.7
  10.7 0.7 copy-start.8

commit v3 on v2

--- a/solution.py
+++ b/solution.py
@@ -19,6 +19,7 @@
 F32 = jnp.float32
 FAR_FIRST = (4, 5, 3, 6, 2, 7, 1)
 N_WIRES = 176
+VMEM_BYTES = 60 * 1024 * 1024
 
 
 def dot(a, b):
@@ -112,6 +113,8 @@
     g_ref,
     own_ref,
     z_out,
+    z_half,
+    pair_out,
     z_in,
     fin_out,
     fin_ref,
@@ -161,7 +164,7 @@
 
     loads["hidden"].wait()
     loads["ld"].wait()
-    hid = hidden_ref[...]
+    hid = hidden_ref[...].T
     rot = dot(hid, ld_ref[:, LATENT:])
     rot = jnp.concatenate([rot, jnp.zeros_like(rot)], axis=1)
     kv_y = []
@@ -174,15 +177,48 @@
     kv_own[:, 0:128] = dot(hid, ld_ref[:, l_cols])
     kv_own[:, 128:256] = rot
     loads["qd"].wait()
-    q_y = []
     for d in (2, 1, 3):
         q_out[d - 1] = dot(hid, qd_ref[:, rows(ys[d] * 384, 384)]).astype(BF16)
-        q_y.append(wires.send(q_out.at[d - 1], q_in.at[d - 1], to_y[d]))
     q_own[...] = dot(hid, qd_ref[:, q_cols])
 
+    def over_y(copies, own, received):
+        wait_all(copies)
+        total = own[...]
+        for d in range(NY - 1):
+            total = total + received[d].astype(F32)
+        own[...] = total
+        return total
+
+    def to_all_z(total, out, received):
+        for i in range(NZ):
+            out[i] = total[16 * i : 16 * i + 16].astype(BF16)
+        return [wires.send(out.at[zs[d]], received.at[d - 1], to_z[d]) for d in FAR_FIRST]
+
+    here = rows(z * 16, 16)
+
+    def over_z(copies, own, received):
+        wait_all(copies)
+        total = own[here, :]
+        for d in range(NZ - 1):
+            total = total + received[d].astype(F32)
+        return total
+
+    def square(i, values):
+        total = jnp.sum(values * values, axis=1, keepdims=True)
+        sq_out[i] = jnp.broadcast_to(total, (16, 128))
+        return [wires.send(sq_out.at[i], sq_in.at[i, d - 1], to_y[d]) for d in (2, 1, 3)]
+
+    def scale_of(i, copies, count):
+        wait_all(copies)
+        total = sq_out[i] + sq_in[i, 0] + sq_in[i, 1] + sq_in[i, 2]
+        return lax.rsqrt(total[:, 0:1] / count + 1e-06)
+
+    kv_z = to_all_z(over_y(kv_y, kv_own, kv_in), kvz_out, kvz_in)
+    q_y = [wires.send(q_out.at[d - 1], q_in.at[d - 1], to_y[d]) for d in (2, 1, 3)]
     loads["pos"].wait()
     loads["freq"].wait()
-    angles = freq_ref[...] * pos_ref[...].astype(F32)[None, :]
+    freq = jnp.broadcast_to(freq_ref[...][None, :], (128, 128)).T[: ROPE // 2]
+    angles = freq * pos_ref[...].astype(F32)[None, :]
     cosine, sine = jnp.cos(angles), jnp.sin(angles)
     cos_ref[...] = jnp.concatenate([cosine, cosine, cosine, cosine], axis=0).T
     sin_ref[...] = jnp.concatenate([-sine, sine, -sine, sine], axis=0).T
@@ -191,40 +227,6 @@
     gain_ref[...] = qg_ref[...][None, :]
     lgain_ref[...] = lg_ref[...][None, :]
 
-    def over_y(copies, own, received):
-        wait_all(copies)
-        total = own[...]
-        for d in range(NY - 1):
-            total = total + received[d].astype(F32)
-        own[...] = total
-        return total
-
-    def to_all_z(total, out, received):
-        for i in range(NZ):
-            out[i] = total[16 * i : 16 * i + 16].astype(BF16)
-        return [wires.send(out.at[zs[d]], received.at[d - 1], to_z[d]) for d in FAR_FIRST]
-
-    here = rows(z * 16, 16)
-
-    def over_z(copies, own, received):
-        wait_all(copies)
-        total = own[here, :]
-        for d in range(NZ - 1):
-            total = total + received[d].astype(F32)
-        return total
-
-    def square(i, values):
-        total = jnp.sum(values * values, axis=1, keepdims=True)
-        sq_out[i] = jnp.broadcast_to(total, (16, 128))
-        return [wires.send(sq_out.at[i], sq_in.at[i, d - 1], to_y[d]) for d in (2, 1, 3)]
-
-    def scale_of(i, copies, count):
-        wait_all(copies)
-        total = sq_out[i] + sq_in[i, 0] + sq_in[i, 1] + sq_in[i, 2]
-        return lax.rsqrt(total[:, 0:1] / count + 1e-06)
-
-    kv_z = to_all_z(over_y(kv_y, kv_own, kv_in), kvz_out, kvz_in)
-    q_z = to_all_z(over_y(q_y, q_own, q_in), qz_out, qz_in)
     mine = over_z(kv_z, kv_own, kvz_in)
     lat, rot = mine[:, :128], mine[:, 128:]
     kv_sq = square(0, lat)
@@ -232,18 +234,13 @@
     swapped = jnp.concatenate([rot[:, half:ROPE], rot[:, :half]], axis=1)
     turned = rot[:, :ROPE] * cos_ref[here, :ROPE] + swapped * sin_ref[here, :ROPE]
     kz_ref[zh, here, 128:256] = jnp.concatenate([turned, jnp.zeros_like(turned)], axis=1).astype(BF16)
-    q_low = over_z(q_z, q_own, qz_in)
-    q_sq = square(1, q_low)
-
+    q_total = over_y(q_y, q_own, q_in)
     l_scale = scale_of(0, kv_sq, LATENT)
     kz_ref[zh, here, 0:128] = (lat * l_scale * lgain_ref[:, l_cols]).astype(BF16)
     piece = kz_ref.at[zh, here]
     kz = [wires.send(piece, piece, to_z[d]) for d in FAR_FIRST]
     kz += [wires.send(piece, piece, to_far[d]) for d in range(NZ)]
-    q_scale = scale_of(1, q_sq, QRANK)
-    q_ref[here, q_cols] = (q_low * q_scale * gain_ref[:, q_cols]).astype(BF16)
-    piece = q_ref.at[here, q_cols]
-    qz = [wires.send(piece, piece, to_z[d]) for d in FAR_FIRST]
+    q_z = to_all_z(q_total, qz_out, qz_in)
 
     def key_rows(d, i):
         return rows(ctx_of(lax.rem(x + NX - d, NX), i, core) * 128, 128)
@@ -265,19 +262,23 @@
             piece = k_ref.at[key_rows(0, 1), cols]
             second_x[d].append(wires.send(piece, piece, to_x[d]))
     second_y[0] = key_over_y(0, 1)
-    wait_all(qz)
-    piece = q_ref.at[:, q_cols]
-    q_all = [wires.send(piece, piece, to_y[d]) for d in (2, 1, 3)]
+    q_low = over_z(q_z, q_own, qz_in)
+    q_sq = square(1, q_low)
     wait_all(first_y)
     first_x = {}
     for d in (2, 1, 3):
         piece = k_ref.at[key_rows(0, 0), :]
         first_x[d] = [wires.send(piece, piece, to_x[d])]
+    q_scale = scale_of(1, q_sq, QRANK)
+    q_ref[here, q_cols] = (q_low * q_scale * gain_ref[:, q_cols]).astype(BF16)
+    piece = q_ref.at[here, q_cols]
+    qz = [wires.send(piece, piece, to_z[d]) for d in FAR_FIRST]
     for d in (1, 3, 2):
         wait_all(second_x[d])
         second_y[d] = key_over_y(d, 1)
-    loads["wo"].wait()
-    weights = [wires.send(wo_ref.at[y], wo_ref.at[y], to_y[d]) for d in (2, 1, 3)]
+    wait_all(qz)
+    piece = q_ref.at[:, q_cols]
+    q_all = [wires.send(piece, piece, to_y[d]) for d in (2, 1, 3)]
 
     key_core = {}
 
@@ -292,8 +293,8 @@
 
     for name in ("qup", "ka", "va", "doc"):
         loads[name].wait()
+    key_to_core(0)
     wait_all(q_all)
-    key_to_core(0)
     full = dot(q_ref[...], qup_ref[...])
     cosine, sine = cos_ref[:, :ROPE], sin_ref[:, :ROPE]
     for h in range(4):
@@ -330,6 +331,8 @@
     key_to_core(3)
     scores(1)
     key_to_core(2)
+    loads["wo"].wait()
+    weights = [wires.send(wo_ref.at[y], wo_ref.at[y], to_y[d]) for d in (2, 1, 3)]
     scores(3)
     scores(2)
 
@@ -371,6 +374,8 @@
     def launch(pair, copies):
         wait_all(copies)
         piece = block(pair, here_zc, 0)
+        if pair:
+            over_far[0].wait_send()
         over_far[pair] = wires.send(piece, piece, to_far[0])
         over_core.append(spread(pair, here_zc, over_x))
 
@@ -379,7 +384,9 @@
     launch(0, handed)
     launch(1, second)
     for pair in range(2):
-        over_far[pair].wait()
+        if pair:
+            over_far[pair].wait_send()
+        over_far[pair].wait_recv()
         over_core.append(spread(pair, far_zc, over_x))
     for pair in range(2):
         for zc in (here_zc, far_zc):
@@ -391,31 +398,33 @@
     wait_all(weights)
 
     pair_at, odd = z // 2, z % 2
-    sums = {}
+    near = (ctx, y * NZ + pair_at * 2 + 1 - odd)
+    halves, sums = {}, {}
     for k in (2, 1, 3, 0):
         zc = lax.rem(pair_at + k, 4)
         total = jnp.zeros((128, out_ref.shape[1]), F32)
         for pair in range(2):
             tokens = g_ref[pair, zc].reshape(128, 1024)
             for i in range(NY):
-                total = total + dot(
-                    tokens[:, 256 * i : 256 * i + 256], wo_ref[i, 256 * pair : 256 * pair + 256, :]
+                total = total + dot_t(
+                    tokens[:, 256 * i : 256 * i + 256], wo_ref[i, :, 256 * pair : 256 * pair + 256]
                 )
         for side in range(2):
             part = total[64 * side : 64 * side + 64]
             part = jnp.concatenate([part[:32], part[32:]], axis=1)
+            own_ref[k, side] = part
             z_out[k, side] = part.astype(BF16)
-            if k == 0:
-                own_ref[side] = part
-        for flip in (0, 1):
-            if k or flip:
-                side = odd + flip - 2 * odd * flip
-                to = (ctx, y * NZ + zc * 2 + side)
-                sums[k, flip] = wires.send(z_out.at[k, side], z_in.at[k, flip], to)
-    total = own_ref[odd]
-    for key in ((0, 1), (1, 0), (1, 1), (3, 0), (3, 1), (2, 0), (2, 1)):
-        sums[key].wait()
-        total = total + z_in[key].astype(F32)
+        halves[k] = wires.send(z_out.at[k, 1 - odd], z_half.at[k], near)
+    for k in (2, 1, 3):
+        halves[k].wait()
+        pair_out[k] = (own_ref[k, odd] + z_half[k].astype(F32)).astype(BF16)
+        to = (ctx, y * NZ + lax.rem(pair_at + k, 4) * 2 + odd)
+        sums[k] = wires.send(pair_out.at[k], z_in.at[k], to)
+    halves[0].wait()
+    total = own_ref[0, odd] + z_half[0].astype(F32)
+    for k in (1, 3, 2):
+        sums[k].wait()
+        total = total + z_in[k].astype(F32)
     width = out_ref.shape[1]
     result = jnp.concatenate([total[:, :width], total[:, width:]], axis=0).astype(BF16)
     for i in range(NX):
@@ -441,9 +450,10 @@
     positions,
 ):
     half = ROPE // 2
-    freqs = 10000.0 ** (-2.0 * np.arange(half) / ROPE)
-    freqs = np.broadcast_to(freqs.astype(np.float32)[:, None], (half, 128))
+    freqs = np.zeros((128,), np.float32)
+    freqs[:half] = 10000.0 ** (-2.0 * np.arange(half) / ROPE)
     width = out_proj.shape[1]
+    hidden, out_proj = hidden.T, out_proj.T
     vmem = pltpu.VMEM
     operands = (
         hidden,
@@ -485,9 +495,11 @@
         vmem((512, 2048), F32),
         vmem((2, 4, 2, 16, 256), BF16),
         vmem((2, 4, 2, 4, 16, 1024), BF16),
-        vmem((2, 32, 2 * width), F32),
+        vmem((4, 2, 32, 2 * width), F32),
         vmem((4, 2, 32, 2 * width), BF16),
-        vmem((4, 2, 32, 2 * width), BF16),
+        vmem((4, 32, 2 * width), BF16),
+        vmem((4, 32, 2 * width), BF16),
+        vmem((4, 32, 2 * width), BF16),
         vmem((4, 16, width), BF16),
         vmem((4, 16, width), BF16),
         pltpu.SemaphoreType.DMA((len(operands),)),
@@ -501,7 +513,7 @@
         out_specs=pl.BlockSpec(memory_space=pltpu.VMEM),
         scratch_shapes=scratch,
         compiler_params=pltpu.CompilerParams(
-            collective_id=0, has_side_effects=True, vmem_limit_bytes=48 * 1024 * 1024
+            collective_id=0, has_side_effects=True, vmem_limit_bytes=VMEM_BYTES
         ),
         name="latent_attention",
     )(*operands)

time: 139 us -> 134 us (0.964)
  local copies, waits for them, and re-layouts: 12 us -> 1.47 us
  Pallas kernels: 126 us -> 132 us
    unnamed x21 -> x1, local copies, waits for them, and re-layouts: 11.3 us -> 1.47 us
    pallas_call x1, Pallas kernels: 126 us -> 132 us  [body(): pl.pallas_call(kernel, out_shape=jax.ShapeDtypeStruct((64, width), BF16),...]
where the time goes in v3:
time: 134 us; the launch traced here: 133 us
  Pallas kernels  132 us (99%)
  local copies, waits for them, and re-layouts  1.47 us (1%)
    pallas_call x1, Pallas kernels, body(): pl.pallas_call(kernel, out_shape=jax.ShapeDtypeStruct((64, width), BF16),...  132 us

profile of v3, /device:TPU:1, one launch (start us, length us, event | category | flops | bytes accessed | tf_op | source)
XLA Modules:
  0.0 133.3 jit_solution(7232224096524135116)
XLA Ops:
  0.0 131.8 %latent_attention.1 = bf16[64,448]{1,0:T(8,128)(2,1)} custom-call(bf16[224,128]{1,0:T(8,128)(2,1)} %bitcast.3, bf16[224,1536]{1,0:T(8,128)(2,1)} %qd_hbm.1, bf16[224,576]{1,0:T(8,128)(2,1)} %ld_hbm.1, f32[1536]{0:T(1024)} %qg_hbm.1, f32[512]{0:T(512)} %lg_hbm.1, bf16[1536,768]{1,0:T(8,128)(2,1)} %qup_hbm.1, bf16[512,512]{1,0:T(8,128)(2,1)} %ka_hbm.1, ...), custom_call_target="tpu_custom_call" | custom-call | tf_op jit(solution)/shard_map/latent_attention/pallas_call | solution.py:509
  131.8 1.5 %copy.14 = bf16[64,448]{1,0:T(8,128)(2,1)} copy(bf16[64,448]{1,0:T(8,128)(2,1)} %latent_attention.1) | data formatting | bytes 114688

commit v4 on v3

--- a/solution.py
+++ b/solution.py
@@ -241,6 +241,15 @@
     kz = [wires.send(piece, piece, to_z[d]) for d in FAR_FIRST]
     kz += [wires.send(piece, piece, to_far[d]) for d in range(NZ)]
     q_z = to_all_z(q_total, qz_out, qz_in)
+    loads["wo"].wait()
+    weights = []
+
+    def share_weights(i):
+        size = wo_ref.shape[1] // 4
+        piece = wo_ref.at[y, i * size : i * size + size, :]
+        weights.extend(wires.send(piece, piece, to_y[d]) for d in (2, 1, 3))
+
+    share_weights(0)
 
     def key_rows(d, i):
         return rows(ctx_of(lax.rem(x + NX - d, NX), i, core) * 128, 128)
@@ -295,6 +304,7 @@
         loads[name].wait()
     key_to_core(0)
     wait_all(q_all)
+    share_weights(1)
     full = dot(q_ref[...], qup_ref[...])
     cosine, sine = cos_ref[:, :ROPE], sin_ref[:, :ROPE]
     for h in range(4):
@@ -331,15 +341,13 @@
     key_to_core(3)
     scores(1)
     key_to_core(2)
-    loads["wo"].wait()
-    weights = [wires.send(wo_ref.at[y], wo_ref.at[y], to_y[d]) for d in (2, 1, 3)]
     scores(3)
     scores(2)
 
     here_zc, far_zc = zh * 2 + core, other * 2 + core
     cols = rows(y * 256, 256)
 
-    def mix(pair):
+    def mix(pair, between):
         mine = slice(pair * 256, pair * 256 + 256)
         most = jnp.concatenate([top[2 * pair], top[2 * pair + 1]], axis=0)
         weighted = jnp.zeros((256, LATENT), F32)
@@ -348,6 +356,7 @@
             expo = jnp.exp(s_ref[mine, 512 * j : 512 * j + 512] - most)
             total = total + jnp.sum(expo, axis=1, keepdims=True)
             weighted = weighted + dot(expo.astype(BF16), k_ref[512 * j : 512 * j + 512, :LATENT])
+        between()
         mixed = (weighted / total).astype(BF16)
         for i in range(2):
             at = (2 * pair + i) * VDIM
@@ -379,10 +388,11 @@
         over_far[pair] = wires.send(piece, piece, to_far[0])
         over_core.append(spread(pair, here_zc, over_x))
 
-    handed = mix(0)
-    second = mix(1)
-    launch(0, handed)
+    handed = mix(0, lambda: None)
+    second = mix(1, lambda: launch(0, handed))
     launch(1, second)
+    share_weights(2)
+    share_weights(3)
     for pair in range(2):
         if pair:
             over_far[pair].wait_send()

time: 134 us -> 117 us (0.87)
  the two profiles are of different devices: /device:TPU:1 before, /device:TPU:8 now
where the time goes in v4:
time: 117 us
  Pallas kernels  116 us (99%)
  local copies, waits for them, and re-layouts  1.47 us (1%)
    pallas_call x1, Pallas kernels, body(): pl.pallas_call(kernel, out_shape=jax.ShapeDtypeStruct((64, width), BF16),...  116 us

profile of v4, /device:TPU:8, one launch (start us, length us, event | category | flops | bytes accessed | tf_op | source)
XLA Modules:
  0.0 117.1 jit_solution(10756469976746416959)
XLA Ops:
  0.0 115.7 %latent_attention.1 = bf16[64,448]{1,0:T(8,128)(2,1)} custom-call(bf16[224,128]{1,0:T(8,128)(2,1)} %bitcast.3, bf16[224,1536]{1,0:T(8,128)(2,1)} %qd_hbm.1, bf16[224,576]{1,0:T(8,128)(2,1)} %ld_hbm.1, f32[1536]{0:T(1024)} %qg_hbm.1, f32[512]{0:T(512)} %lg_hbm.1, bf16[1536,768]{1,0:T(8,128)(2,1)} %qup_hbm.1, bf16[512,512]{1,0:T(8,128)(2,1)} %ka_hbm.1, ...), custom_call_target="tpu_custom_call" | custom-call | tf_op jit(solution)/shard_map/latent_attention/pallas_call | solution.py:519
  115.7 1.5 %copy.14 = bf16[64,448]{1,0:T(8,128)(2,1)} copy(bf16[64,448]{1,0:T(8,128)(2,1)} %latent_attention.1) | data formatting | bytes 114688

commit v5 on v4

--- a/solution.py
+++ b/solution.py
@@ -102,13 +102,12 @@
     kvz_in,
     qz_out,
     qz_in,
-    sq_out,
-    sq_in,
     kz_ref,
     q_ref,
     k_ref,
     qc_ref,
     s_ref,
+    factor_ref,
     ho_ref,
     g_ref,
     own_ref,
@@ -203,16 +202,6 @@
             total = total + received[d].astype(F32)
         return total
 
-    def square(i, values):
-        total = jnp.sum(values * values, axis=1, keepdims=True)
-        sq_out[i] = jnp.broadcast_to(total, (16, 128))
-        return [wires.send(sq_out.at[i], sq_in.at[i, d - 1], to_y[d]) for d in (2, 1, 3)]
-
-    def scale_of(i, copies, count):
-        wait_all(copies)
-        total = sq_out[i] + sq_in[i, 0] + sq_in[i, 1] + sq_in[i, 2]
-        return lax.rsqrt(total[:, 0:1] / count + 1e-06)
-
     kv_z = to_all_z(over_y(kv_y, kv_own, kv_in), kvz_out, kvz_in)
     q_y = [wires.send(q_out.at[d - 1], q_in.at[d - 1], to_y[d]) for d in (2, 1, 3)]
     loads["pos"].wait()
@@ -229,18 +218,15 @@
 
     mine = over_z(kv_z, kv_own, kvz_in)
     lat, rot = mine[:, :128], mine[:, 128:]
-    kv_sq = square(0, lat)
     half = ROPE // 2
     swapped = jnp.concatenate([rot[:, half:ROPE], rot[:, :half]], axis=1)
     turned = rot[:, :ROPE] * cos_ref[here, :ROPE] + swapped * sin_ref[here, :ROPE]
     kz_ref[zh, here, 128:256] = jnp.concatenate([turned, jnp.zeros_like(turned)], axis=1).astype(BF16)
-    q_total = over_y(q_y, q_own, q_in)
-    l_scale = scale_of(0, kv_sq, LATENT)
-    kz_ref[zh, here, 0:128] = (lat * l_scale * lgain_ref[:, l_cols]).astype(BF16)
+    kz_ref[zh, here, 0:128] = lat.astype(BF16)
     piece = kz_ref.at[zh, here]
     kz = [wires.send(piece, piece, to_z[d]) for d in FAR_FIRST]
     kz += [wires.send(piece, piece, to_far[d]) for d in range(NZ)]
-    q_z = to_all_z(q_total, qz_out, qz_in)
+    q_z = to_all_z(over_y(q_y, q_own, q_in), qz_out, qz_in)
     loads["wo"].wait()
     weights = []
 
@@ -272,16 +258,14 @@
             second_x[d].append(wires.send(piece, piece, to_x[d]))
     second_y[0] = key_over_y(0, 1)
     q_low = over_z(q_z, q_own, qz_in)
-    q_sq = square(1, q_low)
+    q_ref[here, q_cols] = (q_low * gain_ref[:, q_cols]).astype(BF16)
+    piece = q_ref.at[here, q_cols]
+    qz = [wires.send(piece, piece, to_z[d]) for d in FAR_FIRST]
     wait_all(first_y)
     first_x = {}
     for d in (2, 1, 3):
         piece = k_ref.at[key_rows(0, 0), :]
         first_x[d] = [wires.send(piece, piece, to_x[d])]
-    q_scale = scale_of(1, q_sq, QRANK)
-    q_ref[here, q_cols] = (q_low * q_scale * gain_ref[:, q_cols]).astype(BF16)
-    piece = q_ref.at[here, q_cols]
-    qz = [wires.send(piece, piece, to_z[d]) for d in FAR_FIRST]
     for d in (1, 3, 2):
         wait_all(second_x[d])
         second_y[d] = key_over_y(d, 1)
@@ -305,7 +289,10 @@
     key_to_core(0)
     wait_all(q_all)
     share_weights(1)
-    full = dot(q_ref[...], qup_ref[...])
+    plain = q_ref[...].astype(F32) / gain_ref[...]
+    mean = jnp.sum(plain * plain, axis=1, keepdims=True) / QRANK
+    full = dot(q_ref[...], qup_ref[...]) * lax.rsqrt(mean + 1e-06)
+    lgain = lgain_ref[...]
     cosine, sine = cos_ref[:, :ROPE], sin_ref[:, :ROPE]
     for h in range(4):
         at = h * (NOPE + ROPE)
@@ -315,7 +302,7 @@
         turned = raw * cosine + swapped * sine
         low = dot_t(nope, ka_ref[:, h * NOPE : (h + 1) * NOPE])
         mine = slice(h * 128, h * 128 + 128)
-        qc_ref[mine, :LATENT] = low.astype(BF16)
+        qc_ref[mine, :LATENT] = (low * lgain).astype(BF16)
         qc_ref[mine, LATENT:] = jnp.concatenate([turned, jnp.zeros_like(turned)], axis=1).astype(BF16)
 
     doc = jnp.broadcast_to(doc_ref[...].astype(F32)[None, :], (128, 128)).T[:, 0:1].astype(jnp.int32)
@@ -328,10 +315,17 @@
         at = rows(lax.rem(x + NX - d, NX) * 512, 512)
         key_index = key_lane + lax.rem(x + NX - d, NX) * 512
         bias = jnp.where((key_index <= query_index) & (key_index >= doc), 0.0, -1e30)
-        block = dot_t(qc_ref[...], k_ref[at, :])
+        keys = k_ref[at, :LATENT]
+        wide = keys.astype(F32)
+        mean = dot_t(jnp.ones((8, LATENT), BF16), (wide * wide).astype(BF16)) / LATENT
+        factor = lax.rsqrt(mean + 1e-06)
+        factor_ref[:, at] = factor
+        factor = factor[0:1] * SCALE
+        block = dot_t(qc_ref[:, :LATENT], keys)
+        turn = dot_t(qc_ref[:, LATENT:], k_ref[at, LATENT:])
         for h in range(4):
             mine = slice(h * 128, h * 128 + 128)
-            values = block[mine] * SCALE + bias
+            values = block[mine] * factor + (turn[mine] * SCALE + bias)
             s_ref[mine, at] = values
             most = jnp.max(values, axis=1, keepdims=True)
             top[h] = most if top[h] is None else jnp.maximum(top[h], most)
@@ -353,11 +347,13 @@
         weighted = jnp.zeros((256, LATENT), F32)
         total = jnp.zeros((256, 1), F32)
         for j in range(4):
-            expo = jnp.exp(s_ref[mine, 512 * j : 512 * j + 512] - most)
+            span = slice(512 * j, 512 * j + 512)
+            expo = jnp.exp(s_ref[mine, span] - most)
             total = total + jnp.sum(expo, axis=1, keepdims=True)
-            weighted = weighted + dot(expo.astype(BF16), k_ref[512 * j : 512 * j + 512, :LATENT])
+            expo = expo * factor_ref[0:1, span]
+            weighted = weighted + dot(expo.astype(BF16), k_ref[span, :LATENT])
         between()
-        mixed = (weighted / total).astype(BF16)
+        mixed = (weighted * lgain / total).astype(BF16)
         for i in range(2):
             at = (2 * pair + i) * VDIM
             result = dot(mixed[128 * i : 128 * i + 128], va_ref[:, at : at + VDIM]).astype(BF16)
@@ -383,8 +379,6 @@
     def launch(pair, copies):
         wait_all(copies)
         piece = block(pair, here_zc, 0)
-        if pair:
-            over_far[0].wait_send()
         over_far[pair] = wires.send(piece, piece, to_far[0])
         over_core.append(spread(pair, here_zc, over_x))
 
@@ -394,9 +388,7 @@
     share_weights(2)
     share_weights(3)
     for pair in range(2):
-        if pair:
-            over_far[pair].wait_send()
-        over_far[pair].wait_recv()
+        over_far[pair].wait()
         over_core.append(spread(pair, far_zc, over_x))
     for pair in range(2):
         for zc in (here_zc, far_zc):
@@ -496,13 +488,12 @@
         vmem((7, 16, 256), BF16),
         vmem((8, 16, 384), BF16),
         vmem((7, 16, 384), BF16),
-        vmem((2, 16, 128), F32),
-        vmem((2, 3, 16, 128), F32),
         vmem((2, 128, 256), BF16),
         vmem((128, QRANK), BF16),
         vmem((2048, KEY), BF16),
         vmem((512, KEY), BF16),
         vmem((512, 2048), F32),
+        vmem((8, 2048), F32),
         vmem((2, 4, 2, 16, 256), BF16),
         vmem((2, 4, 2, 4, 16, 1024), BF16),
         vmem((4, 2, 32, 2 * width), F32),

time: 117 us -> 113 us (0.966)
  the two profiles are of different devices: /device:TPU:8 before, /device:TPU:34 now
where the time goes in v5:
time: 113 us
  Pallas kernels  111 us (98%)
  local copies, waits for them, and re-layouts  1.47 us (1%)
    pallas_call x1, Pallas kernels, body(): pl.pallas_call(kernel, out_shape=jax.ShapeDtypeStruct((64, width), BF16),...  111 us

profile of v5, /device:TPU:34, one launch (start us, length us, event | category | flops | bytes accessed | tf_op | source)
XLA Modules:
  0.0 112.8 jit_solution(14029981591832332312)
XLA Ops:
  0.0 111.3 %latent_attention.1 = bf16[64,448]{1,0:T(8,128)(2,1)} custom-call(bf16[224,128]{1,0:T(8,128)(2,1)} %bitcast.3, bf16[224,1536]{1,0:T(8,128)(2,1)} %qd_hbm.1, bf16[224,576]{1,0:T(8,128)(2,1)} %ld_hbm.1, f32[1536]{0:T(1024)} %qg_hbm.1, f32[512]{0:T(512)} %lg_hbm.1, bf16[1536,768]{1,0:T(8,128)(2,1)} %qup_hbm.1, bf16[512,512]{1,0:T(8,128)(2,1)} %ka_hbm.1, ...), custom_call_target="tpu_custom_call" | custom-call | tf_op jit(solution)/shard_map/latent_attention/pallas_call | solution.py:510
  111.3 1.5 %copy.14 = bf16[64,448]{1,0:T(8,128)(2,1)} copy(bf16[64,448]{1,0:T(8,128)(2,1)} %latent_attention.1) | data formatting | bytes 114688

commit v6 on v5

--- a/solution.py
+++ b/solution.py
@@ -18,7 +18,7 @@
 BF16 = jnp.bfloat16
 F32 = jnp.float32
 FAR_FIRST = (4, 5, 3, 6, 2, 7, 1)
-N_WIRES = 176
+N_WIRES = 224
 VMEM_BYTES = 60 * 1024 * 1024
 
 
@@ -338,10 +338,9 @@
     scores(3)
     scores(2)
 
-    here_zc, far_zc = zh * 2 + core, other * 2 + core
     cols = rows(y * 256, 256)
 
-    def mix(pair, between):
+    def mix(pair):
         mine = slice(pair * 256, pair * 256 + 256)
         most = jnp.concatenate([top[2 * pair], top[2 * pair + 1]], axis=0)
         weighted = jnp.zeros((256, LATENT), F32)
@@ -352,7 +351,6 @@
             total = total + jnp.sum(expo, axis=1, keepdims=True)
             expo = expo * factor_ref[0:1, span]
             weighted = weighted + dot(expo.astype(BF16), k_ref[span, :LATENT])
-        between()
         mixed = (weighted * lgain / total).astype(BF16)
         for i in range(2):
             at = (2 * pair + i) * VDIM
@@ -361,52 +359,61 @@
                 for side in range(2):
                     first = 64 * side + 16 * part
                     ho_ref[pair, part, side, :, 128 * i : 128 * i + 128] = result[first : first + 16]
-        g_ref[pair, here_zc, :, x, :, cols] = ho_ref[pair, y]
-        spot = g_ref.at[pair, here_zc, :, x, :, cols]
+        g_ref[pair, core, :, x, :, cols] = ho_ref[pair, y]
+        spot = g_ref.at[pair, core, :, x, :, cols]
         return [wires.send(ho_ref.at[pair, ys[d]], spot, to_y[d]) for d in (2, 1, 3)]
 
-    def block(pair, zc, d):
-        return g_ref.at[pair, zc, :, lax.rem(x + NX - d, NX)]
-
-    def spread(pair, zc, over_x):
-        piece = block(pair, zc, 0)
-        for d in (2, 1, 3):
-            over_x[pair, zc is far_zc, d] = wires.send(piece, piece, to_x[d])
-        return wires.send(piece, piece, to_core)
-
-    over_x, over_core, over_far = {}, [], {}
+    def block(pair, side, d):
+        return g_ref.at[pair, core, side, lax.rem(x + NX - d, NX)]
+
+    def far_block(pair, side, d):
+        return g_ref.at[pair, 2 + core, side, lax.rem(x + NX - d, NX)]
+
+    over_far, over_x, own_core, far_core = {}, {}, [], []
 
     def launch(pair, copies):
         wait_all(copies)
-        piece = block(pair, here_zc, 0)
-        over_far[pair] = wires.send(piece, piece, to_far[0])
-        over_core.append(spread(pair, here_zc, over_x))
-
-    handed = mix(0, lambda: None)
-    second = mix(1, lambda: launch(0, handed))
-    launch(1, second)
+        for side in range(2):
+            over_far[pair, side] = wires.send(
+                block(pair, side, 0), far_block(pair, side, 0), to_far[0]
+            )
+        piece = block(pair, slice(None), 0)
+        for d in (2, 1, 3):
+            over_x[pair, d] = wires.send(piece, piece, to_x[d])
+        own_core.append(wires.send(piece, piece, to_core))
+
+    handed = [mix(0), mix(1)]
+    launch(0, handed[0])
+    launch(1, handed[1])
     share_weights(2)
     share_weights(3)
+
+    def spread(pair):
+        for side in range(2):
+            over_far[pair, side].wait()
+            piece = far_block(pair, side, 0)
+            for d in (2, 1, 3):
+                over_x[pair, side, d] = wires.send(piece, piece, to_x[d])
+            far_core.append(wires.send(piece, piece, to_core))
+
+    spread(0)
     for pair in range(2):
-        over_far[pair].wait()
-        over_core.append(spread(pair, far_zc, over_x))
-    for pair in range(2):
-        for zc in (here_zc, far_zc):
-            for d in (1, 3, 2):
-                over_x[pair, zc is far_zc, d].wait()
-                piece = block(pair, zc, d)
-                over_core.append(wires.send(piece, piece, to_core))
-    wait_all(over_core)
-    wait_all(weights)
+        for d in (1, 3, 2):
+            over_x[pair, d].wait()
+            piece = block(pair, slice(None), d)
+            own_core.append(wires.send(piece, piece, to_core))
+    spread(1)
 
     pair_at, odd = z // 2, z % 2
     near = (ctx, y * NZ + pair_at * 2 + 1 - odd)
-    halves, sums = {}, {}
-    for k in (2, 1, 3, 0):
-        zc = lax.rem(pair_at + k, 4)
+    halves = {}
+    last = wires.used + 8
+    wires.used += 16
+
+    def product(j):
         total = jnp.zeros((128, out_ref.shape[1]), F32)
         for pair in range(2):
-            tokens = g_ref[pair, zc].reshape(128, 1024)
+            tokens = g_ref[pair, j].reshape(128, 1024)
             for i in range(NY):
                 total = total + dot_t(
                     tokens[:, 256 * i : 256 * i + 256], wo_ref[i, :, 256 * pair : 256 * pair + 256]
@@ -414,19 +421,74 @@
         for side in range(2):
             part = total[64 * side : 64 * side + 64]
             part = jnp.concatenate([part[:32], part[32:]], axis=1)
-            own_ref[k, side] = part
-            z_out[k, side] = part.astype(BF16)
-        halves[k] = wires.send(z_out.at[k, 1 - odd], z_half.at[k], near)
-    for k in (2, 1, 3):
-        halves[k].wait()
-        pair_out[k] = (own_ref[k, odd] + z_half[k].astype(F32)).astype(BF16)
-        to = (ctx, y * NZ + lax.rem(pair_at + k, 4) * 2 + odd)
-        sums[k] = wires.send(pair_out.at[k], z_in.at[k], to)
-    halves[0].wait()
-    total = own_ref[0, odd] + z_half[0].astype(F32)
-    for k in (1, 3, 2):
-        sums[k].wait()
-        total = total + z_in[k].astype(F32)
+            own_ref[j, side] = part
+            z_out[j, side] = part.astype(BF16)
+        halves[j] = wires.send(z_out.at[j, 1 - odd], z_half.at[j], near)
+
+    def pair_of(j):
+        return 2 * (zh, other)[j // 2] + j % 2
+
+    def pair_copy(j):
+        away = lax.rem(pair_of(j) - pair_at + 4, 4)
+        copy = pltpu.make_async_remote_copy(
+            src_ref=pair_out.at[j],
+            dst_ref=z_in.at[away],
+            send_sem=send_sems.at[last + j],
+            recv_sem=recv_sems.at[last + away],
+            device_id=(ctx, y * NZ + pair_of(j) * 2 + odd),
+            device_id_type=MESH,
+        )
+        return away, copy
+
+    def pass_on(j):
+        halves[j].wait()
+        total = own_ref[j, odd] + z_half[j].astype(F32)
+        own_ref[j, odd] = total
+        pair_out[j] = total.astype(BF16)
+        away, copy = pair_copy(j)
+
+        @pl.when(away != 0)
+        def _():
+            copy.start()
+
+    def forward(pair):
+        for side in range(2):
+            for d in (1, 3, 2):
+                over_x[pair, side, d].wait()
+                piece = far_block(pair, side, d)
+                far_core.append(wires.send(piece, piece, to_core))
+
+    wait_all(own_core)
+    wait_all(weights)
+    product(0)
+    product(1)
+    forward(0)
+    pass_on(0)
+    pass_on(1)
+    forward(1)
+    wait_all(far_core)
+    product(2)
+    product(3)
+    pass_on(2)
+    pass_on(3)
+    half_at = pair_at // 2
+    total = own_ref[pair_at % 2 + 2 * (half_at + zh - 2 * half_at * zh), odd]
+    for away in (1, 3, 2):
+        pltpu.make_async_remote_copy(
+            src_ref=pair_out.at[0],
+            dst_ref=z_in.at[away],
+            send_sem=send_sems.at[last],
+            recv_sem=recv_sems.at[last + away],
+            device_id=near,
+            device_id_type=MESH,
+        ).wait_recv()
+        total = total + z_in[away].astype(F32)
+    for j in range(4):
+        away, copy = pair_copy(j)
+
+        @pl.when(away != 0)
+        def _(copy=copy):
+            copy.wait_send()
     width = out_ref.shape[1]
     result = jnp.concatenate([total[:, :width], total[:, width:]], axis=0).astype(BF16)
     for i in range(NX):

time: 113 us -> 109 us (0.965)
  the two profiles are of different devices: /device:TPU:34 before, /device:TPU:1 now
where the time goes in v6:
time: 109 us; the launch traced here: 108 us
  Pallas kernels  106 us (97%)
  local copies, waits for them, and re-layouts  1.47 us (1%)
    pallas_call x1, Pallas kernels, body(): pl.pallas_call(kernel, out_shape=jax.ShapeDtypeStruct((64, width), BF16),...  106 us

profile of v6, /device:TPU:1, one launch (start us, length us, event | category | flops | bytes accessed | tf_op | source)
XLA Modules:
  0.0 107.8 jit_solution(3545734948406758280)
XLA Ops:
  0.0 106.3 %latent_attention.1 = bf16[64,448]{1,0:T(8,128)(2,1)} custom-call(bf16[224,128]{1,0:T(8,128)(2,1)} %bitcast.3, bf16[224,1536]{1,0:T(8,128)(2,1)} %qd_hbm.1, bf16[224,576]{1,0:T(8,128)(2,1)} %ld_hbm.1, f32[1536]{0:T(1024)} %qg_hbm.1, f32[512]{0:T(512)} %lg_hbm.1, bf16[1536,768]{1,0:T(8,128)(2,1)} %qup_hbm.1, bf16[512,512]{1,0:T(8,128)(2,1)} %ka_hbm.1, ...), custom_call_target="tpu_custom_call" | custom-call | tf_op jit(solution)/shard_map/latent_attention/pallas_call | solution.py:572
  106.3 1.5 %copy.14 = bf16[64,448]{1,0:T(8,128)(2,1)} copy(bf16[64,448]{1,0:T(8,128)(2,1)} %latent_attention.1) | data formatting | bytes 114688

commit v7 on v6

--- a/solution.py
+++ b/solution.py
@@ -167,7 +167,7 @@
     rot = dot(hid, ld_ref[:, LATENT:])
     rot = jnp.concatenate([rot, jnp.zeros_like(rot)], axis=1)
     kv_y = []
-    for d in (2, 1, 3):
+    for d in (1, 3, 2):
         kv_out[d - 1, :, 0:128] = dot(hid, ld_ref[:, rows(ys[d] * 128, 128)]).astype(BF16)
         kv_out[d - 1, :, 128:256] = rot.astype(BF16)
         kv_y.append(wires.send(kv_out.at[d - 1], kv_in.at[d - 1], to_y[d]))
@@ -176,7 +176,7 @@
     kv_own[:, 0:128] = dot(hid, ld_ref[:, l_cols])
     kv_own[:, 128:256] = rot
     loads["qd"].wait()
-    for d in (2, 1, 3):
+    for d in (1, 3, 2):
         q_out[d - 1] = dot(hid, qd_ref[:, rows(ys[d] * 384, 384)]).astype(BF16)
     q_own[...] = dot(hid, qd_ref[:, q_cols])
 
@@ -203,7 +203,7 @@
         return total
 
     kv_z = to_all_z(over_y(kv_y, kv_own, kv_in), kvz_out, kvz_in)
-    q_y = [wires.send(q_out.at[d - 1], q_in.at[d - 1], to_y[d]) for d in (2, 1, 3)]
+    q_y = [wires.send(q_out.at[d - 1], q_in.at[d - 1], to_y[d]) for d in (1, 3, 2)]
     loads["pos"].wait()
     loads["freq"].wait()
     freq = jnp.broadcast_to(freq_ref[...][None, :], (128, 128)).T[: ROPE // 2]
@@ -233,9 +233,10 @@
     def share_weights(i):
         size = wo_ref.shape[1] // 4
         piece = wo_ref.at[y, i * size : i * size + size, :]
-        weights.extend(wires.send(piece, piece, to_y[d]) for d in (2, 1, 3))
+        weights.extend(wires.send(piece, piece, to_y[d]) for d in (1, 3, 2))
 
     share_weights(0)
+    share_weights(1)
 
     def key_rows(d, i):
         return rows(ctx_of(lax.rem(x + NX - d, NX), i, core) * 128, 128)
@@ -247,11 +248,11 @@
 
     def key_over_y(d, i):
         piece = k_ref.at[key_rows(d, i), l_cols]
-        return [wires.send(piece, piece, to_y[e]) for e in (2, 1, 3)]
+        return [wires.send(piece, piece, to_y[e]) for e in (1, 3, 2)]
 
     first_y = key_over_y(0, 0)
     second_x, second_y = {}, {}
-    for d in (2, 1, 3):
+    for d in (1, 3, 2):
         second_x[d] = []
         for cols in (l_cols, pl.ds(LATENT, 128)):
             piece = k_ref.at[key_rows(0, 1), cols]
@@ -263,15 +264,15 @@
     qz = [wires.send(piece, piece, to_z[d]) for d in FAR_FIRST]
     wait_all(first_y)
     first_x = {}
-    for d in (2, 1, 3):
+    for d in (1, 3, 2):
         piece = k_ref.at[key_rows(0, 0), :]
         first_x[d] = [wires.send(piece, piece, to_x[d])]
+    wait_all(qz)
+    piece = q_ref.at[:, q_cols]
+    q_all = [wires.send(piece, piece, to_y[d]) for d in (1, 3, 2)]
     for d in (1, 3, 2):
         wait_all(second_x[d])
         second_y[d] = key_over_y(d, 1)
-    wait_all(qz)
-    piece = q_ref.at[:, q_cols]
-    q_all = [wires.send(piece, piece, to_y[d]) for d in (2, 1, 3)]
 
     key_core = {}
 
@@ -288,7 +289,6 @@
         loads[name].wait()
     key_to_core(0)
     wait_all(q_all)
-    share_weights(1)
     plain = q_ref[...].astype(F32) / gain_ref[...]
     mean = jnp.sum(plain * plain, axis=1, keepdims=True) / QRANK
     full = dot(q_ref[...], qup_ref[...]) * lax.rsqrt(mean + 1e-06)
@@ -361,7 +361,7 @@
                     ho_ref[pair, part, side, :, 128 * i : 128 * i + 128] = result[first : first + 16]
         g_ref[pair, core, :, x, :, cols] = ho_ref[pair, y]
         spot = g_ref.at[pair, core, :, x, :, cols]
-        return [wires.send(ho_ref.at[pair, ys[d]], spot, to_y[d]) for d in (2, 1, 3)]
+        return [wires.send(ho_ref.at[pair, ys[d]], spot, to_y[d]) for d in (1, 3, 2)]
 
     def block(pair, side, d):
         return g_ref.at[pair, core, side, lax.rem(x + NX - d, NX)]
@@ -378,7 +378,7 @@
                 block(pair, side, 0), far_block(pair, side, 0), to_far[0]
             )
         piece = block(pair, slice(None), 0)
-        for d in (2, 1, 3):
+        for d in (1, 3, 2):
             over_x[pair, d] = wires.send(piece, piece, to_x[d])
         own_core.append(wires.send(piece, piece, to_core))
 
@@ -392,7 +392,7 @@
         for side in range(2):
             over_far[pair, side].wait()
             piece = far_block(pair, side, 0)
-            for d in (2, 1, 3):
+            for d in (1, 3, 2):
                 over_x[pair, side, d] = wires.send(piece, piece, to_x[d])
             far_core.append(wires.send(piece, piece, to_core))
 
@@ -494,7 +494,7 @@
     for i in range(NX):
         fin_out[i] = result[16 * i : 16 * i + 16]
     fin_ref[y] = fin_out[y]
-    wait_all([wires.send(fin_out.at[ys[d]], fin_ref.at[y], to_y[d]) for d in (2, 1, 3)])
+    wait_all([wires.send(fin_out.at[ys[d]], fin_ref.at[y], to_y[d]) for d in (1, 3, 2)])
     for i in range(NY):
         out_ref[16 * i : 16 * i + 16, :] = fin_ref[i]
     assert wires.used <= N_WIRES

time: 109 us -> 103 us (0.945)
  Pallas kernels: 106 us -> 101 us
    pallas_call x1, Pallas kernels: 106 us -> 101 us  [body(): pl.pallas_call(kernel, out_shape=jax.ShapeDtypeStruct((64, width), BF16),...]
where the time goes in v7:
time: 103 us
  Pallas kernels  101 us (98%)
  local copies, waits for them, and re-layouts  1.47 us (1%)
    pallas_call x1, Pallas kernels, body(): pl.pallas_call(kernel, out_shape=jax.ShapeDtypeStruct((64, width), BF16),...  101 us

profile of v7, /device:TPU:1, one launch (start us, length us, event | category | flops | bytes accessed | tf_op | source)
XLA Modules:
  0.0 102.5 jit_solution(9189864457607029341)
XLA Ops:
  0.0 101.1 %latent_attention.1 = bf16[64,448]{1,0:T(8,128)(2,1)} custom-call(bf16[224,128]{1,0:T(8,128)(2,1)} %bitcast.3, bf16[224,1536]{1,0:T(8,128)(2,1)} %qd_hbm.1, bf16[224,576]{1,0:T(8,128)(2,1)} %ld_hbm.1, f32[1536]{0:T(1024)} %qg_hbm.1, f32[512]{0:T(512)} %lg_hbm.1, bf16[1536,768]{1,0:T(8,128)(2,1)} %qup_hbm.1, bf16[512,512]{1,0:T(8,128)(2,1)} %ka_hbm.1, ...), custom_call_target="tpu_custom_call" | custom-call | tf_op jit(solution)/shard_map/latent_attention/pallas_call | solution.py:572
  101.1 1.5 %copy.14 = bf16[64,448]{1,0:T(8,128)(2,1)} copy(bf16[64,448]{1,0:T(8,128)(2,1)} %latent_attention.1) | data formatting | bytes 114688

commit v8 on v7

--- a/solution.py
+++ b/solution.py
@@ -287,7 +287,8 @@
 
     for name in ("qup", "ka", "va", "doc"):
         loads[name].wait()
-    key_to_core(0)
+    for d in (0, 1, 3, 2):
+        key_to_core(d)
     wait_all(q_all)
     plain = q_ref[...].astype(F32) / gain_ref[...]
     mean = jnp.sum(plain * plain, axis=1, keepdims=True) / QRANK
@@ -330,11 +331,8 @@
             most = jnp.max(values, axis=1, keepdims=True)
             top[h] = most if top[h] is None else jnp.maximum(top[h], most)
 
-    key_to_core(1)
     scores(0)
-    key_to_core(3)
     scores(1)
-    key_to_core(2)
     scores(3)
     scores(2)
 

time: 103 us -> 103 us (level)
  no operation moved by 1% of the time
where the time goes in v8:
time: 103 us; the launch traced here: 102 us
  Pallas kernels  101 us (98%)
  local copies, waits for them, and re-layouts  1.47 us (1%)
    pallas_call x1, Pallas kernels, body(): pl.pallas_call(kernel, out_shape=jax.ShapeDtypeStruct((64, width), BF16),...  101 us

profile of v8, /device:TPU:1, one launch (start us, length us, event | category | flops | bytes accessed | tf_op | source)
XLA Modules:
  0.0 102.5 jit_solution(1538037510474408145)
XLA Ops:
  0.0 101.0 %latent_attention.1 = bf16[64,448]{1,0:T(8,128)(2,1)} custom-call(bf16[224,128]{1,0:T(8,128)(2,1)} %bitcast.3, bf16[224,1536]{1,0:T(8,128)(2,1)} %qd_hbm.1, bf16[224,576]{1,0:T(8,128)(2,1)} %ld_hbm.1, f32[1536]{0:T(1024)} %qg_hbm.1, f32[512]{0:T(512)} %lg_hbm.1, bf16[1536,768]{1,0:T(8,128)(2,1)} %qup_hbm.1, bf16[512,512]{1,0:T(8,128)(2,1)} %ka_hbm.1, ...), custom_call_target="tpu_custom_call" | custom-call | tf_op jit(solution)/shard_map/latent_attention/pallas_call | solution.py:570
  101.0 1.5 %copy.14 = bf16[64,448]{1,0:T(8,128)(2,1)} copy(bf16[64,448]{1,0:T(8,128)(2,1)} %latent_attention.1) | data formatting | bytes 114688
